TPU v7x, 128 devices: a whole 4x4x4 slice. The times are simulated.
128 devices in a mesh: group: 4 (over y_hi, core), fsdp: 32 (over z, y_lo, x).
Axes of the slice: x: 4, y: 4 (y_hi: 2, y_lo: 2; y = y_hi * 2 + y_lo), z: 4, core: 2. Of those that a mesh axis runs over, the one named last changes fastest.
Arguments:
- tokens: bfloat16 [65536, 7168], P(('group', 'fsdp')), may hold values from -6 to 6
- out_grad: bfloat16 [65536, 512], P(('group', 'fsdp')), may hold values from -6 to 6
- proj_weight: bfloat16 [7168, 512], P('fsdp'), may hold values from -0.0625 to 0.0625
- momentum: float32 [4, 896, 4096], P('group', 'fsdp'), may hold values from -6 to 6
- freq_index: int32 [4, 896, 32], P(None, 'fsdp'), may hold values from 0 to 4095, as said below
Outputs:
- latent: bfloat16 [65536, 512], P(('group', 'fsdp'))
- grad_in: bfloat16 [65536, 7168], P(('group', 'fsdp'))
- momentum_out: float32 [4, 896, 4096], P('group', 'fsdp')
- update: float32 [896, 4096], P('fsdp')
Inputs may be any that keep to these rules, and one draw needn't show every extreme that they name: `freq_index`: for each replica and tile the 32 entries are distinct flattened frequencies (row frequency times 64 plus column frequency).
All inputs are finite; a program needn't handle non-finite values.
Results may differ from a plain program's by a relative error of at most 0.00055.
Values may be sent and summed in bfloat16 or wider, within the bound.
A program may use at most 192 MiB of HBM per device.

v0:
```python
import math

import jax
import jax.numpy as jnp
from jax import lax
from jax.sharding import PartitionSpec as P

SIDE = 64


decay_rate = 0.9
highest = lax.Precision.HIGHEST


def cosine_table():
    sample_index = jnp.arange(SIDE, dtype=jnp.float32)
    frequency = sample_index[:, None]
    scaling = jnp.where(frequency == 0, math.sqrt(1.0 / SIDE), math.sqrt(2.0 / SIDE))
    return scaling * jnp.cos(
        math.pi * (2.0 * sample_index[None, :] + 1.0) * frequency / (2.0 * SIDE)
    )


def forward_transform(blocks, cosines):
    halfway = jnp.einsum("ik,ckl->cil", cosines, blocks, precision=highest)
    return jnp.einsum("cil,jl->cij", halfway, cosines, precision=highest)


def inverse_transform(coeffs, cosines):
    halfway = jnp.einsum("ki,ckl->cil", cosines, coeffs, precision=highest)
    return jnp.einsum("cil,lj->cij", halfway, cosines, precision=highest)


def on_device(tokens, out_grad, proj_weight, momentum, freq_index):
    token_count = tokens.shape[0]
    model_width = tokens.shape[1]
    latent_width = proj_weight.shape[1]
    full_weight = lax.all_gather(proj_weight, "fsdp", axis=0, tiled=True)
    latent_sum = jnp.dot(tokens, full_weight, preferred_element_type=jnp.float32)
    grad_in = lax.dot_general(
        out_grad, full_weight, (((1,), (1,)), ((), ())), preferred_element_type=jnp.float32
    ).astype(jnp.bfloat16)
    latent = latent_sum.astype(jnp.bfloat16)
    per_row = latent_width // SIDE
    row_blocks = model_width // SIDE
    grad_blocks = out_grad.reshape(token_count, per_row, SIDE)
    local_tiles = momentum.shape[1]
    token_blocks = tokens.reshape(token_count, row_blocks, SIDE)
    grad_term = jnp.einsum(
        "tri,tcj->rcij", token_blocks, grad_blocks, preferred_element_type=jnp.float32
    )
    grad_term = grad_term.reshape(row_blocks * per_row, SIDE * SIDE)
    summed = lax.psum_scatter(grad_term, "fsdp", scatter_dimension=0, tiled=True)
    grad_scale = 1.0 / math.sqrt(token_count * lax.axis_size("fsdp"))
    accumulated = decay_rate * momentum[0] + grad_scale * summed
    cosines = cosine_table()
    coeffs = forward_transform(accumulated.reshape(local_tiles, SIDE, SIDE), cosines)
    coeffs = coeffs.reshape(local_tiles, SIDE * SIDE)
    own_index = lax.dynamic_index_in_dim(freq_index, lax.axis_index("group"), 0, keepdims=False)
    picked = jnp.take_along_axis(coeffs, own_index, axis=1)
    tile_rows = jnp.arange(local_tiles, dtype=jnp.int32)[:, None]
    own_sparse = jnp.zeros_like(coeffs).at[tile_rows, own_index].add(picked)
    removed = inverse_transform(own_sparse.reshape(local_tiles, SIDE, SIDE), cosines)
    leftover = accumulated - removed.reshape(local_tiles, SIDE * SIDE)
    summed_picks = lax.psum(own_sparse, "group")
    averaged = (summed_picks / lax.axis_size("group")).reshape(local_tiles, SIDE, SIDE)
    update = inverse_transform(averaged, cosines).reshape(local_tiles, SIDE * SIDE)
    return (latent, grad_in, leftover[None], update)


def solution(mesh):
    return jax.shard_map(
        on_device,
        mesh=mesh,
        in_specs=(
            P(("group", "fsdp"), None),
            P(("group", "fsdp"), None),
            P("fsdp", None),
            P("group", "fsdp", None),
            P(None, "fsdp", None),
        ),
        out_specs=(
            P(("group", "fsdp"), None),
            P(("group", "fsdp"), None),
            P("group", "fsdp", None),
            P("fsdp", None),
        ),
        check_vma=False,
    )
```

profile of v0, /device:TPU:0, one launch (start us, length us, event | category | flops | bytes accessed | tf_op | source)
XLA Modules:
  0.0 596.4 jit_solution(5824296506285637851)
XLA Ops:
  8.0 10.5 %copy.46 = bf16[512,7168]{0,1:T(8,128)(2,1)} copy(bf16[512,7168]{1,0:T(8,128)(2,1)} %param.5) | data formatting | bytes 14680064 | tf_op args[0]
  18.7 17.6 %convolution_bitcast_fusion = f32[112,8,64,64]{0,3,2,1:T(8,128)} fusion(bf16[512,8,64,1]{0,2,3,1:T(8,128)(2,1)S(1)} %bitcast.71, bf16[512,112,64]{0,2,1:T(8,128)(2,1)} %bitcast.70), kind=kOutput, calls=%fused_computation.3 | convolution fusion | flops 3758096384 | bytes 22544384 | tf_op jit(solution)/shard_map/tri,tcj->rcij/dot_general | solution.py:49
  36.3 28.1 %copy.48 = f32[112,8,64,64]{3,2,1,0:T(8,128)} copy(f32[112,8,64,64]{0,3,2,1:T(8,128)} %convolution_bitcast_fusion) | data formatting | bytes 29360128 | tf_op jit(solution)/shard_map/tri,tcj->rcij/transpose | solution.py:49
  64.4 24.8 %reshape.93 = f32[896,4096]{1,0:T(8,128)} reshape(f32[112,8,64,64]{3,2,1,0:T(8,128)} %copy.48) | data formatting | bytes 29360128 | tf_op jit(solution)/shard_map/reshape | solution.py:52
  89.2 192.0 %fusion = f32[32,4096]{1,0:T(8,128)S(1)} fusion(f32[896,4096]{1,0:T(8,128)} %reshape.93), kind=kCustom, calls=%all-reduce-scatter | all-reduce-scatter fusion | flops 4194305 | bytes 15204864
  281.2 2.8 collective-permute-start
  284.0 1.3 collective-permute-start.1
  285.3 3.4 collective-permute-start.2
  289.6 4.8 collective-permute-start.3
  295.9 32.2 %collective-permute-done.3 = f32[28,4096]{1,0:T(8,128)S(1)} collective-permute-done((f32[28,4096]{1,0:T(8,128)}, f32[28,4096]{1,0:T(8,128)S(1)}, u32[]{:S(2)}, u32[]{:S(2)}) %collective-permute-start.3) | collective-permute-done | bytes 458784
  328.1 13.3 %concatenate.9 = f32[156,4096]{1,0:T(8,128)} concatenate(f32[28,4096]{1,0:T(8,128)S(1)} %collective-permute-done.3, f32[32,4096]{1,0:T(8,128)S(1)} %collective-permute-done.2, f32[32,4096]{1,0:T(8,128)S(1)} %collective-permute-done.1, f32[32,4096]{1,0:T(8,128)S(1)} %collective-permute-done, f32[32,4096]{1,0:T(8,128)S(1)} %fusion), dimensions={0} | concatenate | bytes 5111808
  341.4 1.6 fusion.3
  343.3 1.6 convolution_bitcast_fusion.3
  344.9 1.6 fusion.10
  346.9 7.3 %gather_fusion = f32[896]{0:T(1024)S(1)} fusion(f32[28,4096]{1,0:T(8,128)S(1)} %reshape.95, s32[896]{0:T(1024)S(1)} %reshape.100), kind=kCustom, calls=%fused_computation | custom fusion | bytes 14336 | tf_op jit(solution)/shard_map/jit(take_along_axis)/gather | solution.py:60
  354.4 46.5 %scatter_fusion = f32[28,4096]{1,0:T(8,128)S(1)} fusion(f32[28,4096]{1,0:T(8,128)S(1)} %broadcast_in_dim.27, s32[896]{0:T(1024)S(1)} %reshape.106, f32[896]{0:T(1024)S(1)} %reshape.108), kind=kCustom, calls=%fused_computation.1 | custom fusion | flops 896 | bytes 17920 | tf_op jit(solution)/shard_map/scatter-add | solution.py:62
  402.6 1.6 convolution_bitcast_fusion.2
  404.2 1.6 fusion.7
  407.5 53.1 %all-reduce.4.cloned.1.call-done = f32[28,4096]{1,0:T(8,128)} async-done(((f32[28,4096]{1,0:T(8,128)}), f32[28,4096]{1,0:T(8,128)}) %all-reduce.4.cloned.1.call-update) | async-done | bytes 458768 | tf_op jit(solution)/shard_map/psum | solution.py:65
  462.0 1.6 convolution_bitcast_fusion.1
  463.7 1.6 fusion.4
  466.4 106.1 %all-gather.2.cloned.1.call-done = bf16[7168,512]{1,0:T(8,128)(2,1)} async-done(((bf16[224,512]{1,0:T(8,128)(2,1)}), bf16[7168,512]{1,0:T(8,128)(2,1)}) %all-gather.2.cloned.1.call-update) | async-done | bytes 7340048 | tf_op jit(solution)/shard_map/all_gather | solution.py:38
  572.6 9.3 %convolution_convert_fusion = bf16[512,7168]{1,0:T(8,128)(2,1)} fusion(bf16[512,512]{1,0:T(8,128)(2,1)S(1)} %copy-done.3, bf16[7168,512]{1,0:T(8,128)(2,1)} %all-gather.2.cloned.1.call-done), kind=kOutput, calls=%fused_computation.2 | convolution fusion | flops 3761766400 | bytes 15204352 | tf_op jit(solution)/shard_map/dot_general | solution.py:40
  581.9 7.0 %convolution_convert_fusion.1 = bf16[512,512]{1,0:T(8,128)(2,1)} fusion(bf16[512,7168]{1,0:T(8,128)(2,1)} %param.5, bf16[7168,512]{1,0:T(8,128)(2,1)S(1)} %copy-done.5), kind=kOutput, calls=%fused_computation.9 | convolution fusion | flops 3758358528 | bytes 15204352 | tf_op jit(solution)/shard_map/dot_general | solution.py:39
  (40 shorter events, 8.5 us)
Async XLA Ops:
  8.0 286.4 %copy-start = (s32[4,28,32]{2,0,1:T(4,128)S(1)}, s32[4,28,32]{2,0,1:T(4,128)}, u32[]{:S(2)}) copy-start(s32[4,28,32]{2,0,1:T(4,128)} %param.9) | copy-start | bytes 43012
  8.0 10.5 %copy-start.3 = (bf16[512,512]{1,0:T(8,128)(2,1)S(1)}, bf16[512,512]{1,0:T(8,128)(2,1)}, u32[]{:S(2)}) copy-start(bf16[512,512]{1,0:T(8,128)(2,1)} %param.6) | copy-start | bytes 1572868
  89.2 205.4 %copy-start.4 = (u32[128]{0:T(128)S(1)}, u32[128]{0:T(128)}, u32[]{:S(2)}) copy-start(u32[128]{0:T(128)} %constant.87) | copy-start | bytes 1540
  281.2 46.9 %collective-permute-start = (f32[32,4096]{1,0:T(8,128)S(1)}, f32[32,4096]{1,0:T(8,128)S(1)}, u32[]{:S(2)}, u32[]{:S(2)}) collective-permute-start(f32[32,4096]{1,0:T(8,128)S(1)} %fusion), channel_id=1, source_target_pairs={{0,1},{1,2},{2,3},{3,4},{4,5},{5,6},{6,7},{7,8},{8,9},{9,10},{10,1... | collective-permute-start | bytes 1572872
  284.0 44.1 %collective-permute-start.1 = (f32[32,4096]{1,0:T(8,128)S(1)}, f32[32,4096]{1,0:T(8,128)S(1)}, u32[]{:S(2)}, u32[]{:S(2)}) collective-permute-start(f32[32,4096]{1,0:T(8,128)S(1)} %fusion), channel_id=1, source_target_pairs={{0,2},{1,3},{2,4},{3,5},{4,6},{5,7},{6,8},{7,9},{8,10},{9,11},{10,... | collective-permute-start | bytes 1572872
  285.3 42.8 %collective-permute-start.2 = (f32[32,4096]{1,0:T(8,128)S(1)}, f32[32,4096]{1,0:T(8,128)S(1)}, u32[]{:S(2)}, u32[]{:S(2)}) collective-permute-start(f32[32,4096]{1,0:T(8,128)S(1)} %fusion), channel_id=1, source_target_pairs={{0,3},{1,4},{2,5},{3,6},{4,7},{5,8},{6,9},{7,10},{8,11},{9,12},{10... | collective-permute-start | bytes 1572872
  289.6 38.5 %collective-permute-start.3 = (f32[28,4096]{1,0:T(8,128)}, f32[28,4096]{1,0:T(8,128)S(1)}, u32[]{:S(2)}, u32[]{:S(2)}) collective-permute-start(f32[28,4096]{1,0:T(8,128)} %slice.4), channel_id=1, source_target_pairs={{0,4},{1,5},{2,6},{3,7},{4,8},{5,9},{6,10},{7,11},{8,12},{9,13},{1... | collective-permute-start | bytes 1376264
  400.9 0.8 copy-start.2
  401.3 59.3 %all-reduce.4.cloned.1.call-start = ((), (), s32[]{:S(2)}) async-start(), calls=%async_computation.1 | async-start | bytes 1048576 | tf_op jit(solution)/shard_map/psum | solution.py:65
  402.0 170.6 %all-gather.2.cloned.1.call-start = ((), (), s32[]{:S(2)}) async-start(), calls=%async_computation | async-start | bytes 7569408 | tf_op jit(solution)/shard_map/all_gather | solution.py:38
  572.6 9.3 %copy-start.5 = (bf16[7168,512]{1,0:T(8,128)(2,1)S(1)}, bf16[7168,512]{1,0:T(8,128)(2,1)}, u32[]{:S(2)}) copy-start(bf16[7168,512]{1,0:T(8,128)(2,1)} %all-gather.2.cloned.1.call-done) | copy-start | bytes 22020100
  581.9 7.1 %copy-start.1 = (s32[4,28,32]{2,0,1:T(4,128)S(1)}, s32[4,28,32]{2,0,1:T(4,128)}, u32[]{:S(2)}) copy-start(s32[4,28,32]{2,0,1:T(4,128)} %param.9) | copy-start | bytes 43012
Sparse Core Ops, SparseCore 0:
  405.2 55.3 all-reduce.3
Sparse Core Ops, SparseCore 1:
  404.1 168.4 all-gather.1
where the time goes:
time: 598 us; the launch traced here: 596 us
  blocking collectives  192 us (32%)
  waiting for transfers between devices  192 us (32%)
  local copies, waits for them, and re-layouts  90.4 us (15%)
  other arithmetic  49.2 us (8%)
  matrix products  43.8 us (7%)
  between operations  16.3 us (3%)
  starting transfers between devices  12.7 us (2%)
    unnamed x1, blocking collectives  192 us
    all_gather x1, waiting for transfers between devices, on_device(): full_weight = lax.all_gather(proj_weight, 'fsdp', axis=0, tiled=True)  106 us
    psum x1, waiting for transfers between devices, on_device(): summed_picks = lax.psum(own_sparse, 'group')  53.1 us
    scatter-add x1, other arithmetic, on_device(): own_sparse = jnp.zeros_like(coeffs).at[tile_rows, own_index].add(picked)  46.5 us
    unnamed x6, waiting for transfers between devices  32.8 us
    transpose x1, local copies, waits for them, and re-layouts, on_device(): jnp.einsum('tri,tcj->rcij', token_blocks, grad_blocks, preferred_element_...  28.1 us
    unnamed x18, local copies, waits for them, and re-layouts  27 us
    reshape x1, local copies, waits for them, and re-layouts, on_device(): grad_term = grad_term.reshape(row_blocks * per_row, SIDE * SIDE)  24.8 us
  transfers between devices with their start and end apart: 6, of which 3 were waited for; matrix products, arithmetic and copies ran while one was open for 2% of the time, Pallas kernels for 0%

commit v1 on v0

v1 whole, which is shorter than its diff:
```python
import functools
import math

import jax
import jax.numpy as jnp
import numpy as np
from jax import lax
from jax.experimental import pallas as pl
from jax.experimental.pallas import tpu as pltpu
from jax.sharding import PartitionSpec as P

SIDE = 64
HB = 7
DECAY = 0.9
MESH = pl.DeviceIdType.MESH
F32 = jnp.float32
BF16 = jnp.bfloat16
I16 = jnp.int16
TOK, WIDE, KV = 512, 7168, 512


def cosine_tables():
    n = np.arange(SIDE, dtype=np.float64)
    k = n[:, None]
    scale = np.where(k == 0, math.sqrt(1.0 / SIDE), math.sqrt(2.0 / SIDE))
    table = scale * np.cos(math.pi * (2.0 * n[None, :] + 1.0) * k / (2.0 * SIDE))
    t = table.T.astype(np.float32)
    high = t.astype(jnp.bfloat16)
    low = (t - high.astype(np.float32)).astype(jnp.bfloat16)
    return np.concatenate([high, low], axis=0)


def rem4(v):
    return lax.rem(v + 4, 4)


def dot(a, b):
    return jnp.dot(a, b, preferred_element_type=F32)


def dot_nt(a, b):
    return lax.dot_general(a, b, (((1,), (1,)), ((), ())), preferred_element_type=F32)


def split(v):
    high = v.astype(BF16)
    return high, (v - high.astype(F32)).astype(BF16)


def quantize(v, q_ref, s_ref, row):
    a = jnp.max(jnp.max(jnp.abs(v), axis=0), axis=0, keepdims=True)
    m = jnp.maximum(jnp.maximum(a[:, :128], a[:, 128:]), 1e-30)
    s = m * (1.0 / 32760.0)
    inv = 1.0 / s
    inv2 = jnp.concatenate([inv, inv], axis=1)[None]
    q_ref[...] = jnp.round(v * inv2).astype(jnp.int32).astype(I16)
    s_ref[pl.ds(row, 1), :] = s


def dequantize(q_ref, s_ref, row):
    s = s_ref[pl.ds(row, 1), :]
    s2 = jnp.concatenate([s, s], axis=1)[None]
    return q_ref[...].astype(jnp.int32).astype(F32) * s2


def kernel(
    grad_scale,
    tok_ref, og_ref, w_ref, mom_ref, freq_ref, ct_ref,
    w_out, mom_out, upd_out,
    T, TT, O, W, tmp, SQ, SS, RQ, RS, GH, GO, YQ, YS, ZQ, ZS, TQ, TS, VQ, VS, VH, VL, U, PA,
    load_sem, w_sem, ag_send, ag_recv, core_send, core_recv,
    m_send, m_recv, y_send, y_recv, t_send, t_recv, p_send, p_recv,
):
    g = lax.axis_index("group")
    f = lax.axis_index("fsdp")
    c = lax.rem(g, 2)
    yh = lax.div(g, 2)
    z, yl, x = lax.div(f, 8), lax.rem(lax.div(f, 4), 2), lax.rem(f, 4)
    p0 = x * (1 - c) + z * c
    s0 = z * (1 - c) + x * c

    def f_of(p, s, y):
        xx = p * (1 - c) + s * c
        zz = s * (1 - c) + p * c
        return zz * 8 + y * 4 + xx

    def at_ps(dp, ds):
        return (g, f_of(rem4(p0 + dp), rem4(s0 + ds), yl))

    def at_y(dy):
        yy = rem4(yh * 2 + yl + dy)
        return (lax.div(yy, 2) * 2 + c, f_of(p0, s0, lax.rem(yy, 2)))

    sib = (yh * 2 + 1 - c, f)
    far = ((1 - yh) * 2 + c, f)
    far_sib = ((1 - yh) * 2 + 1 - c, f)
    pn = (at_ps(1, 0), at_ps(-1, 0))
    sn = (at_ps(0, 1), at_ps(0, -1))
    yn = (at_y(1), at_y(-1))
    y_pair = (g, f_of(p0, s0, 1 - yl))

    og_load = pltpu.make_async_copy(og_ref, O, load_sem.at[8])
    og_load.start()
    tok_loads = []
    for i in range(8):
        cp = pltpu.make_async_copy(
            tok_ref.at[:, pl.ds(896 * i, 896)], T.at[:, pl.ds(896 * i, 896)], load_sem.at[i]
        )
        cp.start()
        tok_loads.append(cp)
    w_load = pltpu.make_async_copy(w_ref, W.at[f], w_sem.at[0])
    w_load.start()

    barrier = pltpu.get_barrier_semaphore()
    for d in (*pn, *sn, *yn, sib, far, far_sib):
        pl.semaphore_signal(barrier, inc=1, device_id=d, device_id_type=MESH)
    pl.semaphore_wait(barrier, 9)

    sends = []

    def remote(src, dst, ss, rs, dev):
        cp = pltpu.make_async_remote_copy(
            src_ref=src, dst_ref=dst, send_sem=ss, recv_sem=rs, device_id=dev, device_id_type=MESH
        )
        cp.start()
        sends.append(cp)
        return cp

    def fb(j, t):
        return f_of(rem4(p0 + j), rem4(s0 + t), yl)

    def block(fi):
        return W.at[fi, c]

    n_core = [0]
    core_copies = []

    def to_core(fi):
        i = n_core[0]
        n_core[0] += 1
        core_copies.append(remote(block(fi), block(fi), core_send.at[i], core_recv.at[i], sib))

    w_load.wait()
    n_ag = [0]

    def ag(fi, dev):
        i = n_ag[0]
        n_ag[0] += 1
        return remote(block(fi), block(fi), ag_send.at[i], ag_recv.at[i], dev)

    def s_out(j, t):
        return ag(fb(j, t), yn[0] if j in (0, 1) else yn[1])

    a_p = [ag(fb(0, 0), pn[0]), ag(fb(0, 0), pn[1])]
    a_s = {}
    for d in range(2):
        a_s[d, 0] = ag(fb(0, 0), sn[d])
    a_y = [s_out(0, 0)]

    def ag2():
        a_p[0].wait_recv()
        a_p[1].wait_recv()
        a_p.append(ag(fb(3, 0), pn[0]))
        for j in (3, 1):
            for d in range(2):
                a_s[d, j] = ag(fb(j, 0), sn[d])
        for j in (3, 1):
            a_y.append(s_out(j, 0))
            to_core(fb(j, 0))

    def ag3():
        a_p[2].wait_recv()
        for d in range(2):
            a_s[d, 2] = ag(fb(2, 0), sn[d])
        a_y.append(s_out(2, 0))
        to_core(fb(2, 0))

    a_f = []

    def ag4():
        for j in (0, 3, 1, 2):
            for d in range(2):
                a_s[d, j].wait_recv()
        for j in (0, 1):
            a_f.append(ag(fb(j, 3), sn[0]))
        for j in (2, 3):
            a_f.append(ag(fb(j, 1), sn[1]))
        for t in (3, 1):
            for j in range(4):
                a_y.append(s_out(j, t))
                to_core(fb(j, t))

    def ag5():
        for cp in a_f:
            cp.wait_recv()
        for j in range(4):
            a_y.append(s_out(j, 2))
            to_core(fb(j, 2))

    def ag6():
        for cp in a_y:
            cp.wait_recv()
        for j in range(4):
            for t in range(4):
                to_core(f_of(rem4(p0 + j), rem4(s0 + t), 1 - yl))

    def ag7():
        for cp in core_copies:
            cp.wait_recv()

    def transpose(i):
        tok_loads[i].wait()

        @pl.loop(0, 7)
        def _(b):
            col = pl.multiple_of(i * 896 + b * 128, 128)
            TT[pl.ds(col, 128), :] = T[:, pl.ds(col, 128)].T

    def s_off(k):
        return lax.rem(2 + 3 * k + lax.div(k, 2) * (3 - 2 * lax.rem(k, 2)), 4)

    def chunk(dp, k, y):
        fi = f_of(rem4(p0 + dp), rem4(s0 + s_off(k)), y)
        e = lax.rem(fi, 2)
        row = pl.multiple_of(64 * (7 * lax.div(fi, 2) + 3 * e), 64)
        res = dot(TT[pl.ds(row, 256), :], O[...])
        for i in range(4):
            for h in range(2):
                tmp[y, 2 * i + h] = res[64 * i : 64 * i + 64, 256 * h : 256 * h + 256]
        return e

    def half(h):
        return pl.ds(32 * h, 32)

    def send_m(m, d, k):
        def one(src, dst, i):
            pltpu.make_async_remote_copy(
                src_ref=src.at[m, d, k], dst_ref=dst.at[m, d, k], send_sem=m_send.at[m, d, k, i],
                recv_sem=m_recv.at[m, d, k, i], device_id=pn[d], device_id_type=MESH,
            ).start()

        one(SQ, RQ, 0)
        one(SS, RS, 1)

    def copy_m(m, d, k, i):
        src, dst = ((SQ, RQ), (SS, RS))[i]
        return pltpu.make_async_remote_copy(
            src_ref=src.at[m, d, k], dst_ref=dst.at[m, d, k], send_sem=m_send.at[m, d, k, i],
            recv_sem=m_recv.at[m, d, k, i], device_id=pn[d], device_id_type=MESH,
        )

    def recv_m(m, d, k):
        copy_m(m, d, k, 0).wait_recv()
        copy_m(m, d, k, 1).wait_recv()

    def prepare(i):
        fr = freq_ref[i]
        iota = lax.broadcasted_iota(jnp.int32, (64, 128), 0)
        eu = (iota == lax.shift_right_logical(fr, 6)).astype(F32).astype(BF16)
        ev = (iota == (fr & 63)).astype(F32).astype(BF16)
        res = dot(ct_ref[...], jnp.concatenate([eu, ev], axis=1))
        U[i] = res[:64, :128] + res[64:, :128]
        lane = lax.broadcasted_iota(jnp.int32, (64, 128), 1)
        for t in range(4):
            mine = lax.shift_right_logical(lane, 5) == t
            VH[i, 64 * t : 64 * t + 64, :] = jnp.where(mine, res[:64, 128:], 0.0).astype(BF16)
            VL[i, 64 * t : 64 * t + 64, :] = jnp.where(mine, res[64:, 128:], 0.0).astype(BF16)

    for i in range(4):
        transpose(i)
    ag2()
    for i in range(4, 8):
        transpose(i)
    ag3()
    og_load.wait()

    def first(k):
        for y in range(2):
            e = chunk(2, k, y)
            for d in range(2):
                quantize(tmp[y, pl.ds(e, 7), half(d), :], SQ.at[0, d, k, y], SS.at[0, d, k], y)
        for d in range(2):
            send_m(0, d, k)

    pl.loop(0, 2)(first)
    ag4()
    pl.loop(2, 4)(first)
    ag5()

    @pl.loop(0, 4)
    def _(k):
        for d in range(2):
            for y in range(2):
                e = chunk(1 if d == 0 else -1, k, y)
                quantize(tmp[y, pl.ds(e, 7), half(1 - d), :], SQ.at[1, d, k, y], SS.at[1, d, k], y)
                GH[d, k, y] = tmp[y, pl.ds(e, 7), half(d), :]
            send_m(1, d, k)

    @pl.loop(0, 4)
    def _(k):
        for d in range(2):
            recv_m(0, d, k)
            for y in range(2):
                v = GH[d, k, y] + dequantize(RQ.at[0, d, k, y], RS.at[0, d, k], y)
                quantize(v, SQ.at[2, d, k, y], SS.at[2, d, k], y)
            send_m(2, d, k)

    @pl.loop(0, 4)
    def _(k):
        for y in range(2):
            e = chunk(0, k, y)
            GO[k, y] = tmp[y, pl.ds(e, 7)]

    ag6()
    pl.loop(0, 28)(prepare)

    def y_copy(k, i):
        src, dst = ((YQ, ZQ), (YS, ZS))[i]
        return pltpu.make_async_remote_copy(
            src_ref=src.at[k], dst_ref=dst.at[k], send_sem=y_send.at[k, i],
            recv_sem=y_recv.at[k, i], device_id=y_pair, device_id_type=MESH,
        )

    def sum_p(k):
        for d in range(2):
            recv_m(1, d, k)
            recv_m(2, d, k)

        def total(y, d):
            return (
                GO[k, y, :, half(d), :]
                + dequantize(RQ.at[2, d, k, y], RS.at[2, d, k], y)
                + dequantize(RQ.at[1, 1 - d, k, y], RS.at[1, 1 - d, k], y)
            )

        for d in range(2):
            quantize(total(1 - yl, d), YQ.at[k, d], YS.at[k], d)
        y_copy(k, 0).start()
        y_copy(k, 1).start()
        for d in range(2):
            GO[k, 0, :, half(d), :] = total(yl, d)

    def t_copy(m, d, i):
        src, dst = ((TQ, VQ), (TS, VS))[i]
        return pltpu.make_async_remote_copy(
            src_ref=src.at[m, d], dst_ref=dst.at[m, d], send_sem=t_send.at[m, d, i],
            recv_sem=t_recv.at[m, d, i], device_id=sn[d], device_id_type=MESH,
        )

    def sum_y(k):
        y_copy(k, 0).wait_recv()
        y_copy(k, 1).wait_recv()
        return [
            GO[k, 0, :, half(d), :] + dequantize(ZQ.at[k, d], ZS.at[k], d) for d in range(2)
        ]

    def send_t(m, d, v):
        quantize(v, TQ.at[m, d], TS.at[m, d], 0)
        t_copy(m, d, 0).start()
        t_copy(m, d, 1).start()

    def recv_t(m, d):
        t_copy(m, d, 0).wait_recv()
        t_copy(m, d, 1).wait_recv()
        return dequantize(VQ.at[m, d], VS.at[m, d], 0)

    sum_p(0)
    sum_p(1)
    a = sum_y(0)
    for d in range(2):
        send_t(0, d, a[d])
    sum_p(2)
    a = sum_y(1)
    send_t(1, 0, a[1])
    GO[1, 0, :, half(0), :] = a[0]
    sum_p(3)
    send_t(2, 0, GO[1, 0, :, half(0), :] + recv_t(0, 0))
    a = sum_y(2)
    send_t(1, 1, a[0])
    send_t(2, 1, a[1] + recv_t(0, 1))
    ag7()
    w_store = pltpu.make_async_copy(W, w_out, w_sem.at[1])
    w_store.start()
    a = sum_y(3)
    for d in range(2):
        v = a[d] + recv_t(2, d) + recv_t(1, 1 - d)
        GO[0, 0, :, half(d), :] = v * grad_scale + DECAY * mom_ref[:, half(d), :]

    own = g * HB

    @pl.loop(0, HB)
    def _(i):
        xh, xl = split(GO[0, 0, i])
        r = dot(xh, VH[own + i]) + dot(xl, VH[own + i]) + dot(xh, VL[own + i])
        PA[g, i] = jnp.sum(U[own + i] * r, axis=0, keepdims=True)

    peers = (sib, far, far_sib)
    p_copies = [
        pltpu.make_async_remote_copy(
            src_ref=PA.at[g], dst_ref=PA.at[g], send_sem=p_send.at[i], recv_sem=p_recv.at[i],
            device_id=d, device_id_type=MESH,
        )
        for i, d in enumerate(peers)
    ]
    for cp in p_copies:
        cp.start()

    def back(j, i):
        uh, ul = split(U[j * HB + i] * PA[j, i])
        vh, vl = VH[j * HB + i], VL[j * HB + i]
        return dot_nt(uh, vh) + dot_nt(ul, vh) + dot_nt(uh, vl)

    @pl.loop(0, HB)
    def _(i):
        mom_out[i] = GO[0, 0, i] - back(g, i)

    for cp in p_copies:
        cp.wait_recv()

    @pl.loop(0, HB)
    def _(i):
        upd_out[i] = 0.25 * ((back(0, i) + back(1, i)) + (back(2, i) + back(3, i)))

    for cp in p_copies:
        cp.wait_send()
    for cp in sends:
        cp.wait_send()

    @pl.loop(0, 4)
    def _(k):
        for m in range(3):
            for d in range(2):
                copy_m(m, d, k, 0).wait_send()
                copy_m(m, d, k, 1).wait_send()
        y_copy(k, 0).wait_send()
        y_copy(k, 1).wait_send()

    for m in range(3):
        for d in range(2):
            t_copy(m, d, 0).wait_send()
            t_copy(m, d, 1).wait_send()
    w_store.wait()


def on_device(tokens, out_grad, proj_weight, momentum, freq_index):
    grad_scale = 1.0 / math.sqrt(TOK * 32)
    mom = momentum[0].reshape(HB, 4, SIDE, SIDE).transpose(0, 2, 1, 3).reshape(HB, SIDE, 256)
    freq = freq_index.reshape(4 * HB, 1, 128)
    any_spec = pl.BlockSpec(memory_space=pl.ANY)
    vmem = pl.BlockSpec(memory_space=pltpu.VMEM)
    dma = pltpu.SemaphoreType.DMA
    full, mom_out, upd = pl.pallas_call(
        functools.partial(kernel, grad_scale),
        out_shape=(
            jax.ShapeDtypeStruct((32, 2, 112, KV), BF16),
            jax.ShapeDtypeStruct((HB, SIDE, 256), F32),
            jax.ShapeDtypeStruct((HB, SIDE, 256), F32),
        ),
        in_specs=[any_spec, any_spec, any_spec, vmem, vmem, vmem],
        out_specs=(any_spec, vmem, vmem),
        scratch_shapes=[
            pltpu.VMEM((TOK, WIDE), BF16),
            pltpu.VMEM((WIDE, TOK), BF16),
            pltpu.VMEM((TOK, KV), BF16),
            pltpu.VMEM((32, 2, 112, KV), BF16),
            pltpu.VMEM((2, 8, 64, 256), F32),
            pltpu.VMEM((3, 2, 4, 2, HB, 32, 256), I16),
            pltpu.VMEM((3, 2, 4, 2, 128), F32),
            pltpu.VMEM((3, 2, 4, 2, HB, 32, 256), I16),
            pltpu.VMEM((3, 2, 4, 2, 128), F32),
            pltpu.VMEM((2, 4, 2, HB, 32, 256), F32),
            pltpu.VMEM((4, 2, HB, 64, 256), F32),
            pltpu.VMEM((4, 2, HB, 32, 256), I16),
            pltpu.VMEM((4, 2, 128), F32),
            pltpu.VMEM((4, 2, HB, 32, 256), I16),
            pltpu.VMEM((4, 2, 128), F32),
            pltpu.VMEM((3, 2, HB, 32, 256), I16),
            pltpu.VMEM((3, 2, 1, 128), F32),
            pltpu.VMEM((3, 2, HB, 32, 256), I16),
            pltpu.VMEM((3, 2, 1, 128), F32),
            pltpu.VMEM((4 * HB, 256, 128), BF16),
            pltpu.VMEM((4 * HB, 256, 128), BF16),
            pltpu.VMEM((4 * HB, 64, 128), F32),
            pltpu.VMEM((4, HB, 1, 128), F32),
            dma((9,)),
            dma((2,)),
            dma((40,)),
            dma((40,)),
            dma((31,)),
            dma((31,)),
            dma((3, 2, 4, 2)),
            dma((3, 2, 4, 2)),
            dma((4, 2)),
            dma((4, 2)),
            dma((3, 2, 2)),
            dma((3, 2, 2)),
            dma((3,)),
            dma((3,)),
        ],
        compiler_params=pltpu.CompilerParams(
            collective_id=0, has_side_effects=True, vmem_limit_bytes=62 << 20
        ),
        cost_estimate=pl.CostEstimate(
            flops=4 * 10**9, bytes_accessed=24 * 10**6, transcendentals=0
        ),
    )(tokens, out_grad, proj_weight.reshape(2, 112, KV), mom, freq, jnp.asarray(cosine_tables()))
    full = full.reshape(WIDE, KV)
    latent = dot(tokens, full).astype(BF16)
    grad_in = dot_nt(out_grad, full).astype(BF16)

    def to_tiles(v):
        return v.reshape(HB, SIDE, 4, SIDE).transpose(0, 2, 1, 3).reshape(4 * HB, SIDE * SIDE)

    return latent, grad_in, to_tiles(mom_out)[None], to_tiles(upd)


def solution(mesh):
    return jax.shard_map(
        on_device,
        mesh=mesh,
        in_specs=(
            P(("group", "fsdp"), None),
            P(("group", "fsdp"), None),
            P("fsdp", None),
            P("group", "fsdp", None),
            P(None, "fsdp", None),
        ),
        out_specs=(
            P(("group", "fsdp"), None),
            P(("group", "fsdp"), None),
            P("group", "fsdp", None),
            P("fsdp", None),
        ),
        check_vma=False,
    )
```

time: 598 us -> 119 us (0.20)
  blocking collectives: 192 us -> 0 us
  waiting for transfers between devices: 192 us -> 0 us
  Pallas kernels: 0 us -> 80.6 us
  local copies, waits for them, and re-layouts: 90.4 us -> 18.3 us
  other arithmetic: 49.2 us -> 2.12 us
  matrix products: 43.8 us -> 15.6 us
  between operations: 16.3 us -> 0.73 us
  starting transfers between devices: 12.7 us -> 0 us
    unnamed x1 -> x0, blocking collectives: 192 us -> none
    all_gather x1 -> x0, waiting for transfers between devices: 106 us -> none  [on_device(): full_weight = lax.all_gather(proj_weight, 'fsdp', axis=0, tiled=True)]
    pallas_call x0 -> x1, Pallas kernels: none -> 80.6 us  [on_device(): pl.pallas_call(functools.partial(kernel, grad_scale), out_shape=(jax.Shap...]
    psum x1 -> x0, waiting for transfers between devices: 53.1 us -> none  [on_device(): summed_picks = lax.psum(own_sparse, 'group')]
    scatter-add x1 -> x0, other arithmetic: 46.5 us -> none  [on_device(): own_sparse = jnp.zeros_like(coeffs).at[tile_rows, own_index].add(picked)]
    unnamed x6 -> x0, waiting for transfers between devices: 32.8 us -> none
    dot_general x9 -> x2, matrix products: 43.8 us -> 15.6 us  [the longest x1 9.32 us: dot(): return jnp.dot(a, b, preferred_element_type=F32)]
    transpose x1 -> x2, local copies, waits for them, and re-layouts: 28.1 us -> 0.22 us  [to_tiles(): v.reshape(HB, SIDE, 4, SIDE).transpose(0, 2, 1, 3)]
  transfers between devices with their start and end apart: 6 -> 0, of which waited for: 3 -> 0; matrix products, arithmetic and copies ran while one was open for 2% -> 0% of each run, Pallas kernels for 0% -> 0%
where the time goes in v1:
time: 119 us; the launch traced here: 117 us
  Pallas kernels  80.6 us (68%)
  local copies, waits for them, and re-layouts  18.3 us (15%)
  matrix products  15.6 us (13%)
  other arithmetic  2.12 us (2%)
    pallas_call x1, Pallas kernels, on_device(): pl.pallas_call(functools.partial(kernel, grad_scale), out_shape=(jax.Shap...  80.6 us
    unnamed x11, local copies, waits for them, and re-layouts  11.9 us
    dot_general x1, matrix products, dot(): return jnp.dot(a, b, preferred_element_type=F32)  9.32 us
    dot_general x1, matrix products, dot_nt(): lax.dot_general(a, b, (((1,), (1,)), ((), ())), preferred_element_type=F32)  6.29 us

profile of v1, /device:TPU:0, one launch (start us, length us, event | category | flops | bytes accessed | tf_op | source)
XLA Modules:
  0.0 117.4 jit_solution(10932946217934287198)
XLA Ops:
  0.6 0.8 copy.17
  1.5 0.7 reshape.36.freq_ref
  2.2 2.1 %reduce = f32[28,4096]{1,0:T(8,128)S(1)} reduce(f32[1,28,4096]{2,0,1:T(1,128)} %param.9, f32[]{:T(128)} %constant.5), dimensions={0}, to_apply=%param.9.reduce_sub_computation | reduce | bytes 917508 | tf_op args[3]
  4.3 0.4 reshape_squeeze.3
  4.6 0.6 copy.24
  5.2 1.3 %reshape.30.mom_ref = f32[7,64,256]{2,1,0:T(8,128)} reshape(f32[7,64,4,64]{3,2,1,0:T(4,128)S(1)} %bitcast.19) | data formatting | bytes 917504 | tf_op jit(solution)/shard_map/reshape | solution.py:447
  6.6 80.6 %shard_map.93 = (bf16[32,2,112,512]{3,2,1,0:T(8,128)(2,1)}, f32[7,64,256]{2,1,0:T(8,128)}, f32[7,64,256]{2,1,0:T(8,128)}) custom-call(bf16[512,7168]{1,0:T(8,128)(2,1)} %tok_ref.1, bf16[512,512]{1,0:T(8,128)(2,1)} %og_ref.1, bf16[2,112,512]{2,1,0:T(8,128)(2,1)} %bitcast.22, f32[7,64,256]{2,1,0:T(8,128)} %reshape.30.mom_ref, s32[28,1,128]{2,1,0:T(1,128)} %reshape.36.freq_ref, ...), custom_call_target="tpu_custom_call" | custom-call | flops 4000000000 | bytes 24000000 | tf_op jit(solution)/shard_map/pallas_call | solution.py:452
  87.2 0.0 copy-start.2
  87.2 0.0 copy-start.3
  87.2 9.3 %fusion.1 = bf16[512,512]{0,1:T(8,128)(2,1)S(1)} fusion(bf16[7168,512]{1,0:T(8,128)(2,1)} %bitcast.23, bf16[512,7168]{1,0:T(8,128)(2,1)} %tok_ref.1), kind=kOutput, calls=%fused_computation.3 | convolution fusion | flops 3758358528 | bytes 15204352 | tf_op jit(solution)/shard_map/dot_general | solution.py:38
  96.5 0.0 copy-done.2
  96.6 0.0 copy-done.3
  96.6 6.3 %fusion = bf16[512,7168]{0,1:T(8,128)(2,1)} fusion(bf16[7168,512]{1,0:T(8,128)(2,1)S(1)} %bitcast.24, bf16[512,512]{1,0:T(8,128)(2,1)S(1)} %copy-done.2), kind=kOutput, calls=%fused_computation.1 | convolution fusion | flops 3761766400 | bytes 15204352 | tf_op jit(solution)/shard_map/dot_general | solution.py:42
  102.9 0.0 copy-start.1
  102.9 10.0 %copy.22 = bf16[512,7168]{1,0:T(8,128)(2,1)} copy(bf16[512,7168]{0,1:T(8,128)(2,1)} %fusion) | data formatting | bytes 14680064
  112.9 1.0 copy.21
  113.9 0.0 copy-done.1
  113.9 0.4 reshape.33
  114.3 0.1 copy.19
  114.4 1.4 %broadcast_in_dim_reshape.3 = f32[1,28,4096]{2,0,1:T(1,128)} reshape(f32[7,4,64,64]{3,2,1,0:T(8,128)S(1)} %copy.19) | data formatting | bytes 917504 | tf_op jit(solution)/shard_map/broadcast_in_dim;reshape | solution.py:514
  115.7 0.0 copy-done
  115.8 0.4 reshape.34
  116.2 0.1 copy.20
  116.3 1.1 reshape.35
  (1 shorter events, 0.0 us)
Async XLA Ops:
  87.2 9.4 %copy-start.2 = (bf16[512,512]{1,0:T(8,128)(2,1)S(1)}, bf16[512,512]{1,0:T(8,128)(2,1)}, u32[]{:S(2)}) copy-start(bf16[512,512]{1,0:T(8,128)(2,1)} %og_ref.1) | copy-start | bytes 1572868
  87.2 9.4 %copy-start.3 = (bf16[32,2,112,512]{3,2,1,0:T(8,128)(2,1)S(1)}, bf16[32,2,112,512]{3,2,1,0:T(8,128)(2,1)}, u32[]{:S(2)}) copy-start(bf16[32,2,112,512]{3,2,1,0:T(8,128)(2,1)} %get-tuple-element.7) | copy-start | bytes 22020100
  102.9 11.0 %copy-start.1 = (f32[7,64,256]{2,1,0:T(8,128)S(1)}, f32[7,64,256]{2,1,0:T(8,128)}, u32[]{:S(2)}) copy-start(f32[7,64,256]{2,1,0:T(8,128)} %get-tuple-element.8) | copy-start | bytes 1376260
  102.9 12.9 %copy-start = (f32[7,64,256]{2,1,0:T(8,128)S(1)}, f32[7,64,256]{2,1,0:T(8,128)}, u32[]{:S(2)}) copy-start(f32[7,64,256]{2,1,0:T(8,128)} %get-tuple-element.9) | copy-start | bytes 1376260

commit v2 on v1

--- a/solution.py
+++ b/solution.py
@@ -63,11 +63,15 @@
     return q_ref[...].astype(jnp.int32).astype(F32) * s2
 
 
+def lane_low(shape):
+    return lax.broadcasted_iota(jnp.int32, shape, len(shape) - 1) < 64
+
+
 def kernel(
     grad_scale,
     tok_ref, og_ref, w_ref, mom_ref, freq_ref, ct_ref,
-    w_out, mom_out, upd_out,
-    T, TT, O, W, tmp, SQ, SS, RQ, RS, GH, GO, YQ, YS, ZQ, ZS, TQ, TS, VQ, VS, VH, VL, U, PA,
+    w_out, mom_out, upd_out, lat_out,
+    T, TT, O, W, tmp, SQ, SS, RQ, RS, GH, GO, YQ, YS, ZQ, ZS, TQ, TS, VQ, VS, VH, VL, U, PA, MP, MH, FR, LAT,
     load_sem, w_sem, ag_send, ag_recv, core_send, core_recv,
     m_send, m_recv, y_send, y_recv, t_send, t_recv, p_send, p_recv,
 ):
@@ -99,22 +103,28 @@
     yn = (at_y(1), at_y(-1))
     y_pair = (g, f_of(p0, s0, 1 - yl))
 
-    og_load = pltpu.make_async_copy(og_ref, O, load_sem.at[8])
-    og_load.start()
-    tok_loads = []
-    for i in range(8):
-        cp = pltpu.make_async_copy(
-            tok_ref.at[:, pl.ds(896 * i, 896)], T.at[:, pl.ds(896 * i, 896)], load_sem.at[i]
-        )
-        cp.start()
-        tok_loads.append(cp)
-    w_load = pltpu.make_async_copy(w_ref, W.at[f], w_sem.at[0])
-    w_load.start()
-
     barrier = pltpu.get_barrier_semaphore()
     for d in (*pn, *sn, *yn, sib, far, far_sib):
         pl.semaphore_signal(barrier, inc=1, device_id=d, device_id_type=MESH)
-    pl.semaphore_wait(barrier, 9)
+
+    S_OFF = (2, 1, 3, 0)
+
+    og_load = pltpu.make_async_copy(og_ref, O, load_sem.at[8])
+    og_load.start()
+    w_load = pltpu.make_async_copy(w_ref, W.at[f], w_sem.at[0])
+    w_load.start()
+    tok_loads = []
+    for i in range(4):
+        for y in range(2):
+            quad = rem4(z + S_OFF[i]) * 2 + y
+            cols = pl.ds(pl.multiple_of(896 * quad, 128), 896)
+            cp = pltpu.make_async_copy(tok_ref.at[:, cols], T.at[:, cols], load_sem.at[2 * i + y])
+            cp.start()
+            tok_loads.append(cp)
+    mom_load = pltpu.make_async_copy(mom_ref, MP, w_sem.at[2])
+    mom_load.start()
+    freq_load = pltpu.make_async_copy(freq_ref, FR, w_sem.at[3])
+    freq_load.start()
 
     sends = []
 
@@ -132,15 +142,12 @@
     def block(fi):
         return W.at[fi, c]
 
-    n_core = [0]
     core_copies = []
 
     def to_core(fi):
-        i = n_core[0]
-        n_core[0] += 1
+        i = len(core_copies)
         core_copies.append(remote(block(fi), block(fi), core_send.at[i], core_recv.at[i], sib))
 
-    w_load.wait()
     n_ag = [0]
 
     def ag(fi, dev):
@@ -151,11 +158,15 @@
     def s_out(j, t):
         return ag(fb(j, t), yn[0] if j in (0, 1) else yn[1])
 
-    a_p = [ag(fb(0, 0), pn[0]), ag(fb(0, 0), pn[1])]
-    a_s = {}
-    for d in range(2):
-        a_s[d, 0] = ag(fb(0, 0), sn[d])
-    a_y = [s_out(0, 0)]
+    a_p, a_s, a_y, a_f = [], {}, [], []
+
+    def ag1():
+        w_load.wait()
+        for d in range(2):
+            a_p.append(ag(fb(0, 0), pn[d]))
+        for d in range(2):
+            a_s[d, 0] = ag(fb(0, 0), sn[d])
+        a_y.append(s_out(0, 0))
 
     def ag2():
         a_p[0].wait_recv()
@@ -174,8 +185,6 @@
             a_s[d, 2] = ag(fb(2, 0), sn[d])
         a_y.append(s_out(2, 0))
         to_core(fb(2, 0))
-
-    a_f = []
 
     def ag4():
         for j in (0, 3, 1, 2):
@@ -197,50 +206,57 @@
             a_y.append(s_out(j, 2))
             to_core(fb(j, 2))
 
-    def ag6():
-        for cp in a_y:
+    def ag6(first):
+        for cp in a_y[:12] if first else a_y[12:]:
             cp.wait_recv()
-        for j in range(4):
-            for t in range(4):
+        for t in (0, 3, 1) if first else (2,):
+            for j in range(4):
                 to_core(f_of(rem4(p0 + j), rem4(s0 + t), 1 - yl))
 
-    def ag7():
-        for cp in core_copies:
+    def ag7(low, high):
+        for cp in core_copies[low:high]:
             cp.wait_recv()
 
+    def latent_part(y, fresh):
+        @pl.loop(0, 4)
+        def _(i):
+            cols = pl.ds(pl.multiple_of(896 * (2 * i + y), 128), 896)
+            w = W[pl.ds(8 * i + 4 * y, 4)].reshape(896, KV)
+            part = dot(T[:, cols], w)
+            if fresh:
+
+                @pl.when(i == 0)
+                def _():
+                    LAT[...] = part
+
+                @pl.when(i > 0)
+                def _():
+                    LAT[...] += part
+            else:
+                LAT[...] += part
+
     def transpose(i):
-        tok_loads[i].wait()
-
-        @pl.loop(0, 7)
-        def _(b):
-            col = pl.multiple_of(i * 896 + b * 128, 128)
-            TT[pl.ds(col, 128), :] = T[:, pl.ds(col, 128)].T
-
-    def s_off(k):
-        return lax.rem(2 + 3 * k + lax.div(k, 2) * (3 - 2 * lax.rem(k, 2)), 4)
-
-    def chunk(dp, k, y):
-        fi = f_of(rem4(p0 + dp), rem4(s0 + s_off(k)), y)
+        for y in range(2):
+            tok_loads[2 * i + y].wait()
+            quad = rem4(z + S_OFF[i]) * 2 + y
+
+            @pl.loop(0, 7)
+            def _(b):
+                col = pl.multiple_of(quad * 896 + b * 128, 128)
+                TT[pl.ds(col, 128), :] = T[:, pl.ds(col, 128)].T
+
+    def chunk(dp, k, y, slot):
+        fi = f_of(rem4(p0 + dp), rem4(s0 + S_OFF[k]), y)
         e = lax.rem(fi, 2)
         row = pl.multiple_of(64 * (7 * lax.div(fi, 2) + 3 * e), 64)
         res = dot(TT[pl.ds(row, 256), :], O[...])
         for i in range(4):
             for h in range(2):
-                tmp[y, 2 * i + h] = res[64 * i : 64 * i + 64, 256 * h : 256 * h + 256]
+                tmp[slot, 2 * i + h] = res[64 * i : 64 * i + 64, 256 * h : 256 * h + 256]
         return e
 
     def half(h):
         return pl.ds(32 * h, 32)
-
-    def send_m(m, d, k):
-        def one(src, dst, i):
-            pltpu.make_async_remote_copy(
-                src_ref=src.at[m, d, k], dst_ref=dst.at[m, d, k], send_sem=m_send.at[m, d, k, i],
-                recv_sem=m_recv.at[m, d, k, i], device_id=pn[d], device_id_type=MESH,
-            ).start()
-
-        one(SQ, RQ, 0)
-        one(SS, RS, 1)
 
     def copy_m(m, d, k, i):
         src, dst = ((SQ, RQ), (SS, RS))[i]
@@ -249,55 +265,59 @@
             recv_sem=m_recv.at[m, d, k, i], device_id=pn[d], device_id_type=MESH,
         )
 
+    def send_m(m, d, k):
+        copy_m(m, d, k, 0).start()
+        copy_m(m, d, k, 1).start()
+
     def recv_m(m, d, k):
         copy_m(m, d, k, 0).wait_recv()
         copy_m(m, d, k, 1).wait_recv()
 
     def prepare(i):
-        fr = freq_ref[i]
-        iota = lax.broadcasted_iota(jnp.int32, (64, 128), 0)
-        eu = (iota == lax.shift_right_logical(fr, 6)).astype(F32).astype(BF16)
-        ev = (iota == (fr & 63)).astype(F32).astype(BF16)
-        res = dot(ct_ref[...], jnp.concatenate([eu, ev], axis=1))
-        U[i] = res[:64, :128] + res[64:, :128]
-        lane = lax.broadcasted_iota(jnp.int32, (64, 128), 1)
-        for t in range(4):
-            mine = lax.shift_right_logical(lane, 5) == t
-            VH[i, 64 * t : 64 * t + 64, :] = jnp.where(mine, res[:64, 128:], 0.0).astype(BF16)
-            VL[i, 64 * t : 64 * t + 64, :] = jnp.where(mine, res[64:, 128:], 0.0).astype(BF16)
-
-    for i in range(4):
-        transpose(i)
-    ag2()
-    for i in range(4, 8):
-        transpose(i)
-    ag3()
-    og_load.wait()
+        fr4 = jnp.concatenate([FR[4 * i + t] for t in range(4)], axis=1)
+        for j in range(4):
+            fr = fr4[j : j + 1, :]
+            iota = lax.broadcasted_iota(jnp.int32, (64, 128), 0)
+            eu = (iota == lax.shift_right_logical(fr, 6)).astype(F32).astype(BF16)
+            ev = (iota == (fr & 63)).astype(F32).astype(BF16)
+            res = dot(ct_ref[...], jnp.concatenate([eu, ev], axis=1))
+            U[j * HB + i] = res[:64, :128] + res[64:, :128]
+            lane = lax.broadcasted_iota(jnp.int32, (64, 128), 1)
+            for t in range(4):
+                mine = lax.shift_right_logical(lane, 5) == t
+                rows = slice(64 * t, 64 * t + 64)
+                VH[j * HB + i, rows, :] = jnp.where(mine, res[:64, 128:], 0.0).astype(BF16)
+                VL[j * HB + i, rows, :] = jnp.where(mine, res[64:, 128:], 0.0).astype(BF16)
+
+    def unpack_momentum():
+        mom_load.wait()
+        low = lane_low((32, 128))
+
+        @pl.loop(0, HB)
+        def _(i):
+            for v in range(2):
+                a, b = MP[4 * i + 2 * v], MP[4 * i + 2 * v + 1]
+                MH[i, v, pl.ds(0, 32, stride=2), :] = DECAY * jnp.where(low, a, pltpu.roll(b, 64, 1))
+                MH[i, v, pl.ds(1, 32, stride=2), :] = DECAY * jnp.where(low, pltpu.roll(a, 64, 1), b)
 
     def first(k):
         for y in range(2):
-            e = chunk(2, k, y)
+            e = chunk(2, k, y, y)
             for d in range(2):
                 quantize(tmp[y, pl.ds(e, 7), half(d), :], SQ.at[0, d, k, y], SS.at[0, d, k], y)
-        for d in range(2):
-            send_m(0, d, k)
-
-    pl.loop(0, 2)(first)
-    ag4()
-    pl.loop(2, 4)(first)
-    ag5()
-
-    @pl.loop(0, 4)
-    def _(k):
+
+    def second(k):
         for d in range(2):
             for y in range(2):
-                e = chunk(1 if d == 0 else -1, k, y)
-                quantize(tmp[y, pl.ds(e, 7), half(1 - d), :], SQ.at[1, d, k, y], SS.at[1, d, k], y)
-                GH[d, k, y] = tmp[y, pl.ds(e, 7), half(d), :]
+                slot = 2 * d + y
+                e = chunk(1 if d == 0 else -1, k, y, slot)
+                quantize(
+                    tmp[slot, pl.ds(e, 7), half(1 - d), :], SQ.at[1, d, k, y], SS.at[1, d, k], y
+                )
+                GH[d, k, y] = tmp[slot, pl.ds(e, 7), half(d), :]
             send_m(1, d, k)
 
-    @pl.loop(0, 4)
-    def _(k):
+    def third(k):
         for d in range(2):
             recv_m(0, d, k)
             for y in range(2):
@@ -305,14 +325,10 @@
                 quantize(v, SQ.at[2, d, k, y], SS.at[2, d, k], y)
             send_m(2, d, k)
 
-    @pl.loop(0, 4)
-    def _(k):
+    def own_part(k):
         for y in range(2):
-            e = chunk(0, k, y)
+            e = chunk(0, k, y, y)
             GO[k, y] = tmp[y, pl.ds(e, 7)]
-
-    ag6()
-    pl.loop(0, 28)(prepare)
 
     def y_copy(k, i):
         src, dst = ((YQ, ZQ), (YS, ZS))[i]
@@ -364,32 +380,76 @@
         t_copy(m, d, 1).wait_recv()
         return dequantize(VQ.at[m, d], VS.at[m, d], 0)
 
+    def send_first(k):
+        for d in range(2):
+            send_m(0, d, k)
+
+    transpose(0)
+    og_load.wait()
+    first(0)
+    transpose(1)
+    first(1)
+    pl.semaphore_wait(barrier, 9)
+    ag1()
+    send_first(0)
+    send_first(1)
+    transpose(2)
+    first(2)
+    send_first(2)
+    transpose(3)
+    first(3)
+    send_first(3)
+    freq_load.wait()
+    second(0)
+    ag2()
+    second(1)
+    third(0)
+    own_part(0)
+    pl.loop(0, 2)(prepare)
+    ag3()
+    ag4()
+    second(2)
+    third(1)
+    own_part(1)
+    pl.loop(2, 4)(prepare)
+    second(3)
+    third(2)
+    ag5()
     sum_p(0)
+    own_part(2)
+    pl.loop(4, HB)(prepare)
+    third(3)
+    own_part(3)
+    unpack_momentum()
     sum_p(1)
     a = sum_y(0)
     for d in range(2):
         send_t(0, d, a[d])
+    ag6(True)
+    ag7(0, 15)
+    latent_part(yl, True)
     sum_p(2)
     a = sum_y(1)
     send_t(1, 0, a[1])
-    GO[1, 0, :, half(0), :] = a[0]
+    send_t(2, 0, a[0] + recv_t(0, 0))
+    ag6(False)
     sum_p(3)
-    send_t(2, 0, GO[1, 0, :, half(0), :] + recv_t(0, 0))
     a = sum_y(2)
     send_t(1, 1, a[0])
     send_t(2, 1, a[1] + recv_t(0, 1))
-    ag7()
+    ag7(15, 31)
     w_store = pltpu.make_async_copy(W, w_out, w_sem.at[1])
     w_store.start()
+    latent_part(1 - yl, False)
     a = sum_y(3)
     for d in range(2):
         v = a[d] + recv_t(2, d) + recv_t(1, 1 - d)
-        GO[0, 0, :, half(d), :] = v * grad_scale + DECAY * mom_ref[:, half(d), :]
+        for h in range(2):
+            cols = slice(128 * h, 128 * h + 128)
+            GO[0, 0, :, half(d), cols] = v[:, :, cols] * grad_scale + MH[:, h, half(d), :]
 
     own = g * HB
-
-    @pl.loop(0, HB)
-    def _(i):
+    for i in range(HB):
         xh, xl = split(GO[0, 0, i])
         r = dot(xh, VH[own + i]) + dot(xl, VH[own + i]) + dot(xh, VL[own + i])
         PA[g, i] = jnp.sum(U[own + i] * r, axis=0, keepdims=True)
@@ -410,19 +470,14 @@
         vh, vl = VH[j * HB + i], VL[j * HB + i]
         return dot_nt(uh, vh) + dot_nt(ul, vh) + dot_nt(uh, vl)
 
-    @pl.loop(0, HB)
-    def _(i):
-        mom_out[i] = GO[0, 0, i] - back(g, i)
-
-    for cp in p_copies:
-        cp.wait_recv()
-
-    @pl.loop(0, HB)
-    def _(i):
-        upd_out[i] = 0.25 * ((back(0, i) + back(1, i)) + (back(2, i) + back(3, i)))
-
-    for cp in p_copies:
-        cp.wait_send()
+    def put_pair(ref, i, v):
+        ref[i, 0] = v[:, :128]
+        ref[i, 1] = v[:, 128:]
+
+    for i in range(HB):
+        put_pair(mom_out, i, GO[0, 0, i] - back(g, i))
+    lat_out[...] = LAT[...].astype(BF16)
+
     for cp in sends:
         cp.wait_send()
 
@@ -441,29 +496,91 @@
             t_copy(m, d, 1).wait_send()
     w_store.wait()
 
+    for cp in p_copies:
+        cp.wait_recv()
+    for i in range(HB):
+        put_pair(upd_out, i, 0.25 * ((back(0, i) + back(1, i)) + (back(2, i) + back(3, i))))
+    for cp in p_copies:
+        cp.wait_send()
+
+
+def finish_kernel(
+    og_ref, w_ref, mom_ref, upd_ref, lat_ref,
+    grad_out, mom_out, upd_out, lat_out,
+    O, W, G, MI, UI, L, MO, packed, UO, w_sem, g_sem, sem,
+):
+    parts, cols = G.shape[0], G.shape[2]
+
+    def copy(src, dst, s):
+        cp = pltpu.make_async_copy(src, dst, s)
+        cp.start()
+        return cp
+
+    o_load = copy(og_ref, O, sem.at[0])
+    w_loads = [
+        copy(w_ref.at[pl.ds(cols * i, cols)], W.at[pl.ds(cols * i, cols)], w_sem.at[i])
+        for i in range(parts)
+    ]
+    l_load = copy(lat_ref, L, sem.at[1])
+    m_load = copy(mom_ref, MI, sem.at[2])
+    u_load = copy(upd_ref, UI, sem.at[3])
+    stores = []
+    o_load.wait()
+    for i in range(parts):
+        w_loads[i].wait()
+        G[i] = dot_nt(O[...], W[cols * i : cols * i + cols, :]).astype(BF16)
+        stores.append(copy(G.at[i], grad_out.at[:, pl.ds(cols * i, cols)], g_sem.at[i]))
+    l_load.wait()
+    stores.append(copy(L, lat_out, sem.at[4]))
+    low = lane_low((32, 128))
+
+    def pack(ref, put):
+        for i in range(HB):
+            for v in range(2):
+                a = ref[i, v, pl.ds(0, 32, stride=2), :]
+                b = ref[i, v, pl.ds(1, 32, stride=2), :]
+                put(4 * i + 2 * v, jnp.where(low, a, pltpu.roll(b, 64, 1)))
+                put(4 * i + 2 * v + 1, jnp.where(low, pltpu.roll(a, 64, 1), b))
+
+    def put_mom(t, v):
+        MO[t] = v
+
+    def put_upd(t, v):
+        packed[32 * t : 32 * t + 32, :] = v
+
+    m_load.wait()
+    pack(MI, put_mom)
+    stores.append(copy(MO, mom_out, sem.at[5]))
+    u_load.wait()
+    pack(UI, put_upd)
+    for m in range(32):
+        UO[:, 128 * m : 128 * m + 128] = packed[pl.ds(m, 28, stride=32), :]
+    stores.append(copy(UO, upd_out, sem.at[6]))
+    for cp in stores:
+        cp.wait()
+
 
 def on_device(tokens, out_grad, proj_weight, momentum, freq_index):
     grad_scale = 1.0 / math.sqrt(TOK * 32)
-    mom = momentum[0].reshape(HB, 4, SIDE, SIDE).transpose(0, 2, 1, 3).reshape(HB, SIDE, 256)
-    freq = freq_index.reshape(4 * HB, 1, 128)
     any_spec = pl.BlockSpec(memory_space=pl.ANY)
     vmem = pl.BlockSpec(memory_space=pltpu.VMEM)
     dma = pltpu.SemaphoreType.DMA
-    full, mom_out, upd = pl.pallas_call(
+    full, mom_hb, upd_hb, lat = pl.pallas_call(
         functools.partial(kernel, grad_scale),
         out_shape=(
             jax.ShapeDtypeStruct((32, 2, 112, KV), BF16),
-            jax.ShapeDtypeStruct((HB, SIDE, 256), F32),
-            jax.ShapeDtypeStruct((HB, SIDE, 256), F32),
+            jax.ShapeDtypeStruct((HB, 2, SIDE, 128), F32),
+            jax.ShapeDtypeStruct((HB, 2, SIDE, 128), F32),
+            jax.ShapeDtypeStruct((TOK, KV), BF16),
         ),
-        in_specs=[any_spec, any_spec, any_spec, vmem, vmem, vmem],
-        out_specs=(any_spec, vmem, vmem),
+        in_specs=[any_spec, any_spec, any_spec, any_spec, any_spec, vmem],
+        out_specs=(any_spec, vmem, vmem, vmem),
         scratch_shapes=[
             pltpu.VMEM((TOK, WIDE), BF16),
             pltpu.VMEM((WIDE, TOK), BF16),
             pltpu.VMEM((TOK, KV), BF16),
             pltpu.VMEM((32, 2, 112, KV), BF16),
-            pltpu.VMEM((2, 8, 64, 256), F32),
+            pltpu.VMEM((4, 8, 64, 256), F32),
             pltpu.VMEM((3, 2, 4, 2, HB, 32, 256), I16),
             pltpu.VMEM((3, 2, 4, 2, 128), F32),
             pltpu.VMEM((3, 2, 4, 2, HB, 32, 256), I16),
@@ -482,10 +599,14 @@
             pltpu.VMEM((4 * HB, 256, 128), BF16),
             pltpu.VMEM((4 * HB, 64, 128), F32),
             pltpu.VMEM((4, HB, 1, 128), F32),
+            pltpu.VMEM((4 * HB, 32, 128), F32),
+            pltpu.VMEM((HB, 2, SIDE, 128), F32),
+            pltpu.VMEM((4 * HB, 4, 32), jnp.int32),
+            pltpu.VMEM((TOK, KV), F32),
             dma((9,)),
-            dma((2,)),
-            dma((40,)),
-            dma((40,)),
+            dma((4,)),
+            dma((31,)),
+            dma((31,)),
             dma((31,)),
             dma((31,)),
             dma((3, 2, 4, 2)),
@@ -501,17 +622,48 @@
             collective_id=0, has_side_effects=True, vmem_limit_bytes=62 << 20
         ),
         cost_estimate=pl.CostEstimate(
-            flops=4 * 10**9, bytes_accessed=24 * 10**6, transcendentals=0
+            flops=8 * 10**9, bytes_accessed=24 * 10**6, transcendentals=0
         ),
-    )(tokens, out_grad, proj_weight.reshape(2, 112, KV), mom, freq, jnp.asarray(cosine_tables()))
-    full = full.reshape(WIDE, KV)
-    latent = dot(tokens, full).astype(BF16)
-    grad_in = dot_nt(out_grad, full).astype(BF16)
-
-    def to_tiles(v):
-        return v.reshape(HB, SIDE, 4, SIDE).transpose(0, 2, 1, 3).reshape(4 * HB, SIDE * SIDE)
-
-    return latent, grad_in, to_tiles(mom_out)[None], to_tiles(upd)
+    )(
+        tokens,
+        out_grad,
+        proj_weight.reshape(2, 112, KV),
+        momentum.reshape(4 * HB, 32, 128),
+        freq_index.transpose(1, 0, 2),
+        jnp.asarray(cosine_tables()),
+    )
+    parts = 8
+    cols = WIDE // parts
+    grad_in, mom_out, upd, latent = pl.pallas_call(
+        finish_kernel,
+        out_shape=(
+            jax.ShapeDtypeStruct((TOK, WIDE), BF16),
+            jax.ShapeDtypeStruct((4 * HB, 32, 128), F32),
+            jax.ShapeDtypeStruct((4 * HB, SIDE * SIDE), F32),
+            jax.ShapeDtypeStruct((TOK, KV), BF16),
+        ),
+        in_specs=[any_spec] * 5,
+        out_specs=(any_spec,) * 4,
+        scratch_shapes=[
+            pltpu.VMEM((TOK, KV), BF16),
+            pltpu.VMEM((WIDE, KV), BF16),
+            pltpu.VMEM((parts, TOK, cols), BF16),
+            pltpu.VMEM((HB, 2, SIDE, 128), F32),
+            pltpu.VMEM((HB, 2, SIDE, 128), F32),
+            pltpu.VMEM((TOK, KV), BF16),
+            pltpu.VMEM((4 * HB, 32, 128), F32),
+            pltpu.VMEM((28 * 32, 128), F32),
+            pltpu.VMEM((4 * HB, SIDE * SIDE), F32),
+            dma((parts,)),
+            dma((parts,)),
+            dma((7,)),
+        ],
+        compiler_params=pltpu.CompilerParams(vmem_limit_bytes=62 << 20),
+        cost_estimate=pl.CostEstimate(
+            flops=4 * 10**9, bytes_accessed=16 * 10**6, transcendentals=0
+        ),
+    )(out_grad, full.reshape(WIDE, KV), mom_hb, upd_hb, lat)
+    return latent, grad_in, mom_out.reshape(1, 4 * HB, SIDE * SIDE), upd
 
 
 def solution(mesh):

time: 119 us -> 94.5 us (0.79)
  local copies, waits for them, and re-layouts: 18.3 us -> 0 us
  matrix products: 15.6 us -> 0 us
  Pallas kernels: 80.6 us -> 92.5 us
  other arithmetic: 2.12 us -> 0 us
    dot_general x2 -> x0, matrix products: 15.6 us -> none  [the longest x1 9.32 us: dot(): return jnp.dot(a, b, preferred_element_type=F32)]
    unnamed x11 -> x0, local copies, waits for them, and re-layouts: 11.9 us -> none
    pallas_call x0 -> x1, Pallas kernels: none -> 9.68 us  [on_device(): pl.pallas_call(finish_kernel, out_shape=(jax.ShapeDtypeStruct((TOK, WIDE)...]
    reshape x5 -> x0, local copies, waits for them, and re-layouts: 3.92 us -> none  [the longest x3 1.92 us: to_tiles(): v.reshape(HB, SIDE, 4, SIDE).transpose(0, 2, 1, 3)]
    another operation x3 -> x0, local copies, waits for them, and re-layouts: 2.3 us -> none  [the longest x1 1.35 us: on_device(): return (latent, grad_in, to_tiles(mom_out)[None], to_tiles(upd))]
    pallas_call x1, Pallas kernels: 80.6 us -> 82.8 us  [on_device(): pl.pallas_call(functools.partial(kernel, grad_scale), out_shape=(jax.Shap...]
    unnamed x1 -> x0, other arithmetic: 2.12 us -> none
where the time goes in v2:
time: 94.5 us; the launch traced here: 93.3 us
  Pallas kernels  92.5 us (98%)
    pallas_call x1, Pallas kernels, on_device(): pl.pallas_call(functools.partial(kernel, grad_scale), out_shape=(jax.Shap...  82.8 us
    pallas_call x1, Pallas kernels, on_device(): pl.pallas_call(finish_kernel, out_shape=(jax.ShapeDtypeStruct((TOK, WIDE)...  9.68 us

profile of v2, /device:TPU:0, one launch (start us, length us, event | category | flops | bytes accessed | tf_op | source)
XLA Modules:
  0.0 93.3 jit_solution(7182846691735800397)
XLA Ops:
  0.6 82.8 %shard_map.93 = (bf16[32,2,112,512]{3,2,1,0:T(8,128)(2,1)}, f32[7,2,64,128]{3,2,1,0:T(8,128)}, f32[7,2,64,128]{3,2,1,0:T(8,128)}, bf16[512,512]{1,0:T(8,128)(2,1)}) custom-call(bf16[512,7168]{1,0:T(8,128)(2,1)} %tok_ref.1, bf16[512,512]{1,0:T(8,128)(2,1)} %og_ref.3, bf16[2,112,512]{2,1,0:T(8,128)(2,1)} %bitcast.6, f32[28,32,128]{2,1,0:T(8,128)} %bitcast.5, ...), custom_call_target="tpu_custom_call" | custom-call | flops 8000000000 | bytes 24000000 | tf_op jit(solution)/shard_map/pallas_call | solution.py:568
  83.4 9.7 %shard_map.94 = (bf16[512,7168]{1,0:T(8,128)(2,1)}, f32[28,32,128]{2,1,0:T(8,128)}, f32[28,4096]{1,0:T(8,128)}, bf16[512,512]{1,0:T(8,128)(2,1)}) custom-call(bf16[512,512]{1,0:T(8,128)(2,1)} %og_ref.3, bf16[7168,512]{1,0:T(8,128)(2,1)} %bitcast.8, f32[7,2,64,128]{3,2,1,0:T(8,128)} %get-tuple-element.13.mom_ref, ...), custom_call_target="tpu_custom_call" | custom-call | flops 4000000000 | bytes 16000000 | tf_op jit(solution)/shard_map/pallas_call | solution.py:637

commit v3 on v2

--- a/solution.py
+++ b/solution.py
@@ -100,11 +100,12 @@
     far_sib = ((1 - yh) * 2 + 1 - c, f)
     pn = (at_ps(1, 0), at_ps(-1, 0))
     sn = (at_ps(0, 1), at_ps(0, -1))
-    yn = (at_y(1), at_y(-1))
     y_pair = (g, f_of(p0, s0, 1 - yl))
+    y_cross = at_y(2 * yl - 1)
+    p_far = at_ps(2, 0)
 
     barrier = pltpu.get_barrier_semaphore()
-    for d in (*pn, *sn, *yn, sib, far, far_sib):
+    for d in (*pn, p_far, *sn, y_pair, y_cross, sib, far, far_sib):
         pl.semaphore_signal(barrier, inc=1, device_id=d, device_id_type=MESH)
 
     S_OFF = (2, 1, 3, 0)
@@ -156,35 +157,27 @@
         return remote(block(fi), block(fi), ag_send.at[i], ag_recv.at[i], dev)
 
     def s_out(j, t):
-        return ag(fb(j, t), yn[0] if j in (0, 1) else yn[1])
+        return ag(fb(j, t), y_pair if j == 2 else y_cross)
 
     a_p, a_s, a_y, a_f = [], {}, [], []
 
     def ag1():
         w_load.wait()
-        for d in range(2):
-            a_p.append(ag(fb(0, 0), pn[d]))
+        for d in (*pn, p_far):
+            a_p.append(ag(fb(0, 0), d))
         for d in range(2):
             a_s[d, 0] = ag(fb(0, 0), sn[d])
         a_y.append(s_out(0, 0))
 
     def ag2():
-        a_p[0].wait_recv()
-        a_p[1].wait_recv()
-        a_p.append(ag(fb(3, 0), pn[0]))
-        for j in (3, 1):
+        for cp in a_p:
+            cp.wait_recv()
+        for j in (3, 1, 2):
             for d in range(2):
                 a_s[d, j] = ag(fb(j, 0), sn[d])
-        for j in (3, 1):
+        for j in (3, 1, 2):
             a_y.append(s_out(j, 0))
             to_core(fb(j, 0))
-
-    def ag3():
-        a_p[2].wait_recv()
-        for d in range(2):
-            a_s[d, 2] = ag(fb(2, 0), sn[d])
-        a_y.append(s_out(2, 0))
-        to_core(fb(2, 0))
 
     def ag4():
         for j in (0, 3, 1, 2):
@@ -389,7 +382,7 @@
     first(0)
     transpose(1)
     first(1)
-    pl.semaphore_wait(barrier, 9)
+    pl.semaphore_wait(barrier, 10)
     ag1()
     send_first(0)
     send_first(1)
@@ -402,41 +395,39 @@
     freq_load.wait()
     second(0)
     ag2()
+    third(0)
     second(1)
-    third(0)
-    own_part(0)
-    pl.loop(0, 2)(prepare)
-    ag3()
+    third(1)
     ag4()
     second(2)
-    third(1)
+    third(2)
+    own_part(0)
+    sum_p(0)
+    second(3)
+    third(3)
+    ag5()
     own_part(1)
-    pl.loop(2, 4)(prepare)
-    second(3)
-    third(2)
-    ag5()
-    sum_p(0)
+    pl.loop(0, 3)(prepare)
+    sum_p(1)
     own_part(2)
-    pl.loop(4, HB)(prepare)
-    third(3)
-    own_part(3)
-    unpack_momentum()
-    sum_p(1)
+    pl.loop(3, HB)(prepare)
     a = sum_y(0)
     for d in range(2):
         send_t(0, d, a[d])
-    ag6(True)
-    ag7(0, 15)
-    latent_part(yl, True)
+    own_part(3)
+    unpack_momentum()
     sum_p(2)
     a = sum_y(1)
     send_t(1, 0, a[1])
     send_t(2, 0, a[0] + recv_t(0, 0))
-    ag6(False)
+    ag7(0, 15)
+    latent_part(yl, True)
     sum_p(3)
+    ag6(True)
     a = sum_y(2)
     send_t(1, 1, a[0])
     send_t(2, 1, a[1] + recv_t(0, 1))
+    ag6(False)
     ag7(15, 31)
     w_store = pltpu.make_async_copy(W, w_out, w_sem.at[1])
     w_store.start()
@@ -517,21 +508,13 @@
         return cp
 
     o_load = copy(og_ref, O, sem.at[0])
+    m_load = copy(mom_ref, MI, sem.at[2])
+    u_load = copy(upd_ref, UI, sem.at[3])
     w_loads = [
         copy(w_ref.at[pl.ds(cols * i, cols)], W.at[pl.ds(cols * i, cols)], w_sem.at[i])
         for i in range(parts)
     ]
     l_load = copy(lat_ref, L, sem.at[1])
-    m_load = copy(mom_ref, MI, sem.at[2])
-    u_load = copy(upd_ref, UI, sem.at[3])
-    stores = []
-    o_load.wait()
-    for i in range(parts):
-        w_loads[i].wait()
-        G[i] = dot_nt(O[...], W[cols * i : cols * i + cols, :]).astype(BF16)
-        stores.append(copy(G.at[i], grad_out.at[:, pl.ds(cols * i, cols)], g_sem.at[i]))
-    l_load.wait()
-    stores.append(copy(L, lat_out, sem.at[4]))
     low = lane_low((32, 128))
 
     def pack(ref, put):
@@ -548,14 +531,23 @@
     def put_upd(t, v):
         packed[32 * t : 32 * t + 32, :] = v
 
+    stores = []
     m_load.wait()
     pack(MI, put_mom)
     stores.append(copy(MO, mom_out, sem.at[5]))
-    u_load.wait()
-    pack(UI, put_upd)
-    for m in range(32):
-        UO[:, 128 * m : 128 * m + 128] = packed[pl.ds(m, 28, stride=32), :]
-    stores.append(copy(UO, upd_out, sem.at[6]))
+    o_load.wait()
+    for i in range(parts):
+        w_loads[i].wait()
+        G[i] = dot_nt(O[...], W[cols * i : cols * i + cols, :]).astype(BF16)
+        stores.append(copy(G.at[i], grad_out.at[:, pl.ds(cols * i, cols)], g_sem.at[i]))
+        if i == 0:
+            u_load.wait()
+            pack(UI, put_upd)
+            for m in range(32):
+                UO[:, 128 * m : 128 * m + 128] = packed[pl.ds(m, 28, stride=32), :]
+            stores.append(copy(UO, upd_out, sem.at[6]))
+    l_load.wait()
+    stores.append(copy(L, lat_out, sem.at[4]))
     for cp in stores:
         cp.wait()
 
@@ -632,7 +624,7 @@
         freq_index.transpose(1, 0, 2),
         jnp.asarray(cosine_tables()),
     )
-    parts = 8
+    parts = 4
     cols = WIDE // parts
     grad_in, mom_out, upd, latent = pl.pallas_call(
         finish_kernel,

time: 94.5 us -> 82.4 us (0.87)
  Pallas kernels: 92.5 us -> 80.4 us
    pallas_call x1, Pallas kernels: 82.8 us -> 71.4 us  [on_device(): pl.pallas_call(functools.partial(kernel, grad_scale), out_shape=(jax.Shap...]
where the time goes in v3:
time: 82.4 us; the launch traced here: 81.2 us
  Pallas kernels  80.4 us (98%)
    pallas_call x1, Pallas kernels, on_device(): pl.pallas_call(functools.partial(kernel, grad_scale), out_shape=(jax.Shap...  71.4 us
    pallas_call x1, Pallas kernels, on_device(): pl.pallas_call(finish_kernel, out_shape=(jax.ShapeDtypeStruct((TOK, WIDE)...  8.98 us

profile of v3, /device:TPU:0, one launch (start us, length us, event | category | flops | bytes accessed | tf_op | source)
XLA Modules:
  0.0 81.2 jit_solution(9199237729827064819)
XLA Ops:
  0.6 71.4 %shard_map.93 = (bf16[32,2,112,512]{3,2,1,0:T(8,128)(2,1)}, f32[7,2,64,128]{3,2,1,0:T(8,128)}, f32[7,2,64,128]{3,2,1,0:T(8,128)}, bf16[512,512]{1,0:T(8,128)(2,1)}) custom-call(bf16[512,7168]{1,0:T(8,128)(2,1)} %tok_ref.1, bf16[512,512]{1,0:T(8,128)(2,1)} %og_ref.3, bf16[2,112,512]{2,1,0:T(8,128)(2,1)} %bitcast.6, f32[28,32,128]{2,1,0:T(8,128)} %bitcast.5, ...), custom_call_target="tpu_custom_call" | custom-call | flops 8000000000 | bytes 24000000 | tf_op jit(solution)/shard_map/pallas_call | solution.py:560
  72.1 9.0 %shard_map.94 = (bf16[512,7168]{1,0:T(8,128)(2,1)}, f32[28,32,128]{2,1,0:T(8,128)}, f32[28,4096]{1,0:T(8,128)}, bf16[512,512]{1,0:T(8,128)(2,1)}) custom-call(bf16[512,512]{1,0:T(8,128)(2,1)} %og_ref.3, bf16[7168,512]{1,0:T(8,128)(2,1)} %bitcast.8, f32[7,2,64,128]{3,2,1,0:T(8,128)} %get-tuple-element.13.mom_ref, ...), custom_call_target="tpu_custom_call" | custom-call | flops 4000000000 | bytes 16000000 | tf_op jit(solution)/shard_map/pallas_call | solution.py:629

commit v4 on v3

--- a/solution.py
+++ b/solution.py
@@ -72,8 +72,9 @@
     tok_ref, og_ref, w_ref, mom_ref, freq_ref, ct_ref,
     w_out, mom_out, upd_out, lat_out,
     T, TT, O, W, tmp, SQ, SS, RQ, RS, GH, GO, YQ, YS, ZQ, ZS, TQ, TS, VQ, VS, VH, VL, U, PA, MP, MH, FR, LAT,
+    FQ, FS, FZ, FT,
     load_sem, w_sem, ag_send, ag_recv, core_send, core_recv,
-    m_send, m_recv, y_send, y_recv, t_send, t_recv, p_send, p_recv,
+    m_send, m_recv, y_send, y_recv, t_send, t_recv, p_send, p_recv, f_send, f_recv,
 ):
     g = lax.axis_index("group")
     f = lax.axis_index("fsdp")
@@ -108,20 +109,21 @@
     for d in (*pn, p_far, *sn, y_pair, y_cross, sib, far, far_sib):
         pl.semaphore_signal(barrier, inc=1, device_id=d, device_id_type=MESH)
 
-    S_OFF = (2, 1, 3, 0)
+    S_OFF = (2, 1, 0, 3)
+    LATE = 3
 
     og_load = pltpu.make_async_copy(og_ref, O, load_sem.at[8])
     og_load.start()
     w_load = pltpu.make_async_copy(w_ref, W.at[f], w_sem.at[0])
     w_load.start()
-    tok_loads = []
-    for i in range(4):
+    tok_loads = {}
+    for i in (0, 3, 1, 2):
         for y in range(2):
             quad = rem4(z + S_OFF[i]) * 2 + y
             cols = pl.ds(pl.multiple_of(896 * quad, 128), 896)
             cp = pltpu.make_async_copy(tok_ref.at[:, cols], T.at[:, cols], load_sem.at[2 * i + y])
             cp.start()
-            tok_loads.append(cp)
+            tok_loads[2 * i + y] = cp
     mom_load = pltpu.make_async_copy(mom_ref, MP, w_sem.at[2])
     mom_load.start()
     freq_load = pltpu.make_async_copy(freq_ref, FR, w_sem.at[3])
@@ -157,7 +159,7 @@
         return remote(block(fi), block(fi), ag_send.at[i], ag_recv.at[i], dev)
 
     def s_out(j, t):
-        return ag(fb(j, t), y_pair if j == 2 else y_cross)
+        return ag(fb(j, t), y_pair if j == 2 and t != 2 else y_cross)
 
     a_p, a_s, a_y, a_f = [], {}, [], []
 
@@ -253,8 +255,9 @@
 
     def copy_m(m, d, k, i):
         src, dst = ((SQ, RQ), (SS, RS))[i]
+        at = (m, d, k, 0) if k == LATE and i == 0 else (m, d, k)
         return pltpu.make_async_remote_copy(
-            src_ref=src.at[m, d, k], dst_ref=dst.at[m, d, k], send_sem=m_send.at[m, d, k, i],
+            src_ref=src.at[at], dst_ref=dst.at[at], send_sem=m_send.at[m, d, k, i],
             recv_sem=m_recv.at[m, d, k, i], device_id=pn[d], device_id_type=MESH,
         )
 
@@ -318,6 +321,73 @@
                 quantize(v, SQ.at[2, d, k, y], SS.at[2, d, k], y)
             send_m(2, d, k)
 
+    def f_copy(i, j):
+        src, dst = ((FQ, FZ), (FS, FT))[j]
+        return pltpu.make_async_remote_copy(
+            src_ref=src.at[i], dst_ref=dst.at[i], send_sem=f_send.at[i, j],
+            recv_sem=f_recv.at[i, j], device_id=y_pair, device_id_type=MESH,
+        )
+
+    F_AT = {2: 0, 1: 1, -1: 2, 0: 3}
+
+    def y_first(dp):
+        i = F_AT[dp]
+        e = chunk(dp, LATE, 1 - yl, i)
+        for h in range(2):
+            quantize(tmp[i, pl.ds(e, 7), half(h), :], FQ.at[i, h], FS.at[i], h)
+
+    def send_f(dp):
+        for j in range(2):
+            f_copy(F_AT[dp], j).start()
+
+    def late_part(dp):
+        i = F_AT[dp]
+        e = chunk(dp, LATE, yl, i)
+        for j in range(2):
+            f_copy(i, j).wait_recv()
+        return [
+            tmp[i, pl.ds(e, 7), half(h), :] + dequantize(FZ.at[i, h], FT.at[i], h)
+            for h in range(2)
+        ]
+
+    def put_late(m, d, v):
+        quantize(v, SQ.at[m, d, LATE, 0], SS.at[m, d, LATE], 0)
+        SS[m, d, LATE, pl.ds(1, 1), :] = jnp.zeros((1, 128), F32)
+        send_m(m, d, LATE)
+
+    def late_first():
+        v = late_part(2)
+        for d in range(2):
+            put_late(0, d, v[d])
+
+    def late_second():
+        for d in range(2):
+            v = late_part(1 if d == 0 else -1)
+            put_late(1, d, v[1 - d])
+            GH[d, LATE, 0] = v[d]
+
+    def late_third():
+        for d in range(2):
+            recv_m(0, d, LATE)
+            v = GH[d, LATE, 0] + dequantize(RQ.at[0, d, LATE, 0], RS.at[0, d, LATE], 0)
+            put_late(2, d, v)
+
+    def late_own():
+        v = late_part(0)
+        for h in range(2):
+            GO[LATE, 0, :, half(h), :] = v[h]
+
+    def late_sum():
+        for d in range(2):
+            recv_m(1, d, LATE)
+            recv_m(2, d, LATE)
+        return [
+            GO[LATE, 0, :, half(d), :]
+            + dequantize(RQ.at[2, d, LATE, 0], RS.at[2, d, LATE], 0)
+            + dequantize(RQ.at[1, 1 - d, LATE, 0], RS.at[1, 1 - d, LATE], 0)
+            for d in range(2)
+        ]
+
     def own_part(k):
         for y in range(2):
             e = chunk(0, k, y, y)
@@ -380,22 +450,28 @@
     transpose(0)
     og_load.wait()
     first(0)
-    transpose(1)
-    first(1)
+    transpose(3)
+    y_first(2)
     pl.semaphore_wait(barrier, 10)
     ag1()
     send_first(0)
+    send_f(2)
+    transpose(1)
+    first(1)
     send_first(1)
     transpose(2)
     first(2)
     send_first(2)
-    transpose(3)
-    first(3)
-    send_first(3)
+    for d in (1, -1):
+        y_first(d)
+        send_f(d)
     freq_load.wait()
+    ag2()
     second(0)
-    ag2()
+    y_first(0)
+    send_f(0)
     third(0)
+    late_first()
     second(1)
     third(1)
     ag4()
@@ -403,8 +479,8 @@
     third(2)
     own_part(0)
     sum_p(0)
-    second(3)
-    third(3)
+    late_second()
+    late_third()
     ag5()
     own_part(1)
     pl.loop(0, 3)(prepare)
@@ -414,25 +490,20 @@
     a = sum_y(0)
     for d in range(2):
         send_t(0, d, a[d])
-    own_part(3)
+    late_own()
     unpack_momentum()
     sum_p(2)
     a = sum_y(1)
     send_t(1, 0, a[1])
     send_t(2, 0, a[0] + recv_t(0, 0))
+    a = late_sum()
+    send_t(1, 1, a[0])
+    send_t(2, 1, a[1] + recv_t(0, 1))
     ag7(0, 15)
     latent_part(yl, True)
-    sum_p(3)
     ag6(True)
+    ag6(False)
     a = sum_y(2)
-    send_t(1, 1, a[0])
-    send_t(2, 1, a[1] + recv_t(0, 1))
-    ag6(False)
-    ag7(15, 31)
-    w_store = pltpu.make_async_copy(W, w_out, w_sem.at[1])
-    w_store.start()
-    latent_part(1 - yl, False)
-    a = sum_y(3)
     for d in range(2):
         v = a[d] + recv_t(2, d) + recv_t(1, 1 - d)
         for h in range(2):
@@ -467,19 +538,25 @@
 
     for i in range(HB):
         put_pair(mom_out, i, GO[0, 0, i] - back(g, i))
+    ag7(15, 31)
+    w_store = pltpu.make_async_copy(W, w_out, w_sem.at[1])
+    w_store.start()
+    latent_part(1 - yl, False)
     lat_out[...] = LAT[...].astype(BF16)
 
     for cp in sends:
         cp.wait_send()
 
-    @pl.loop(0, 4)
-    def _(k):
+    for k in range(4):
         for m in range(3):
             for d in range(2):
                 copy_m(m, d, k, 0).wait_send()
                 copy_m(m, d, k, 1).wait_send()
-        y_copy(k, 0).wait_send()
-        y_copy(k, 1).wait_send()
+        if k != LATE:
+            y_copy(k, 0).wait_send()
+            y_copy(k, 1).wait_send()
+        f_copy(k, 0).wait_send()
+        f_copy(k, 1).wait_send()
 
     for m in range(3):
         for d in range(2):
@@ -595,6 +672,10 @@
             pltpu.VMEM((HB, 2, SIDE, 128), F32),
             pltpu.VMEM((4 * HB, 4, 32), jnp.int32),
             pltpu.VMEM((TOK, KV), F32),
+            pltpu.VMEM((4, 2, HB, 32, 256), I16),
+            pltpu.VMEM((4, 2, 128), F32),
+            pltpu.VMEM((4, 2, HB, 32, 256), I16),
+            pltpu.VMEM((4, 2, 128), F32),
             dma((9,)),
             dma((4,)),
             dma((31,)),
@@ -609,6 +690,8 @@
             dma((3, 2, 2)),
             dma((3,)),
             dma((3,)),
+            dma((4, 2)),
+            dma((4, 2)),
         ],
         compiler_params=pltpu.CompilerParams(
             collective_id=0, has_side_effects=True, vmem_limit_bytes=62 << 20

time: 82.4 us -> 75.9 us (0.921)
  Pallas kernels: 80.4 us -> 73.9 us
    pallas_call x1, Pallas kernels: 71.4 us -> 64.9 us  [on_device(): pl.pallas_call(functools.partial(kernel, grad_scale), out_shape=(jax.Shap...]
where the time goes in v4:
time: 75.9 us; the launch traced here: 74.7 us
  Pallas kernels  73.9 us (97%)
  between operations  0.8 us (1%)
    pallas_call x1, Pallas kernels, on_device(): pl.pallas_call(functools.partial(kernel, grad_scale), out_shape=(jax.Shap...  64.9 us
    pallas_call x1, Pallas kernels, on_device(): pl.pallas_call(finish_kernel, out_shape=(jax.ShapeDtypeStruct((TOK, WIDE)...  8.98 us

profile of v4, /device:TPU:0, one launch (start us, length us, event | category | flops | bytes accessed | tf_op | source)
XLA Modules:
  0.0 74.7 jit_solution(17991464362540612334)
XLA Ops:
  0.6 64.9 %shard_map.93 = (bf16[32,2,112,512]{3,2,1,0:T(8,128)(2,1)}, f32[7,2,64,128]{3,2,1,0:T(8,128)}, f32[7,2,64,128]{3,2,1,0:T(8,128)}, bf16[512,512]{1,0:T(8,128)(2,1)}) custom-call(bf16[512,7168]{1,0:T(8,128)(2,1)} %tok_ref.1, bf16[512,512]{1,0:T(8,128)(2,1)} %og_ref.3, bf16[2,112,512]{2,1,0:T(8,128)(2,1)} %bitcast.6, f32[28,32,128]{2,1,0:T(8,128)} %bitcast.5, ...), custom_call_target="tpu_custom_call" | custom-call | flops 8000000000 | bytes 24000000 | tf_op jit(solution)/shard_map/pallas_call | solution.py:637
  65.6 9.0 %shard_map.94 = (bf16[512,7168]{1,0:T(8,128)(2,1)}, f32[28,32,128]{2,1,0:T(8,128)}, f32[28,4096]{1,0:T(8,128)}, bf16[512,512]{1,0:T(8,128)(2,1)}) custom-call(bf16[512,512]{1,0:T(8,128)(2,1)} %og_ref.3, bf16[7168,512]{1,0:T(8,128)(2,1)} %bitcast.8, f32[7,2,64,128]{3,2,1,0:T(8,128)} %get-tuple-element.13.mom_ref, ...), custom_call_target="tpu_custom_call" | custom-call | flops 4000000000 | bytes 16000000 | tf_op jit(solution)/shard_map/pallas_call | solution.py:712

commit v5 on v4

--- a/solution.py
+++ b/solution.py
@@ -74,7 +74,7 @@
     T, TT, O, W, tmp, SQ, SS, RQ, RS, GH, GO, YQ, YS, ZQ, ZS, TQ, TS, VQ, VS, VH, VL, U, PA, MP, MH, FR, LAT,
     FQ, FS, FZ, FT,
     load_sem, w_sem, ag_send, ag_recv, core_send, core_recv,
-    m_send, m_recv, y_send, y_recv, t_send, t_recv, p_send, p_recv, f_send, f_recv,
+    m_send, m_recv, y_send, y_recv, t_send, t_recv, p_send, p_recv, f_send, f_recv, ws_sem,
 ):
     g = lax.axis_index("group")
     f = lax.axis_index("fsdp")
@@ -211,6 +211,15 @@
     def ag7(low, high):
         for cp in core_copies[low:high]:
             cp.wait_recv()
+
+    def store_plane(y, base):
+        copies = []
+        for i in range(4):
+            rows = pl.ds(8 * i + 4 * y, 4)
+            cp = pltpu.make_async_copy(W.at[rows], w_out.at[rows], ws_sem.at[base + i])
+            cp.start()
+            copies.append(cp)
+        return copies
 
     def latent_part(y, fresh):
         @pl.loop(0, 4)
@@ -500,6 +509,7 @@
     send_t(1, 1, a[0])
     send_t(2, 1, a[1] + recv_t(0, 1))
     ag7(0, 15)
+    w_stores = store_plane(yl, 0)
     latent_part(yl, True)
     ag6(True)
     ag6(False)
@@ -539,8 +549,7 @@
     for i in range(HB):
         put_pair(mom_out, i, GO[0, 0, i] - back(g, i))
     ag7(15, 31)
-    w_store = pltpu.make_async_copy(W, w_out, w_sem.at[1])
-    w_store.start()
+    w_stores += store_plane(1 - yl, 4)
     latent_part(1 - yl, False)
     lat_out[...] = LAT[...].astype(BF16)
 
@@ -562,7 +571,8 @@
         for d in range(2):
             t_copy(m, d, 0).wait_send()
             t_copy(m, d, 1).wait_send()
-    w_store.wait()
+    for cp in w_stores:
+        cp.wait()
 
     for cp in p_copies:
         cp.wait_recv()
@@ -617,7 +627,7 @@
         w_loads[i].wait()
         G[i] = dot_nt(O[...], W[cols * i : cols * i + cols, :]).astype(BF16)
         stores.append(copy(G.at[i], grad_out.at[:, pl.ds(cols * i, cols)], g_sem.at[i]))
-        if i == 0:
+        if i == parts - 1:
             u_load.wait()
             pack(UI, put_upd)
             for m in range(32):
@@ -692,6 +702,7 @@
             dma((3,)),
             dma((4, 2)),
             dma((4, 2)),
+            dma((8,)),
         ],
         compiler_params=pltpu.CompilerParams(
             collective_id=0, has_side_effects=True, vmem_limit_bytes=62 << 20

time: 75.9 us -> 75.7 us (level)
  no operation moved by 1% of the time
where the time goes in v5:
time: 75.7 us; the launch traced here: 74.5 us
  Pallas kernels  73.7 us (97%)
  between operations  0.8 us (1%)
    pallas_call x1, Pallas kernels, on_device(): pl.pallas_call(functools.partial(kernel, grad_scale), out_shape=(jax.Shap...  65 us
    pallas_call x1, Pallas kernels, on_device(): pl.pallas_call(finish_kernel, out_shape=(jax.ShapeDtypeStruct((TOK, WIDE)...  8.74 us

profile of v5, /device:TPU:0, one launch (start us, length us, event | category | flops | bytes accessed | tf_op | source)
XLA Modules:
  0.0 74.5 jit_solution(11971051919409833265)
XLA Ops:
  0.6 65.0 %shard_map.93 = (bf16[32,2,112,512]{3,2,1,0:T(8,128)(2,1)}, f32[7,2,64,128]{3,2,1,0:T(8,128)}, f32[7,2,64,128]{3,2,1,0:T(8,128)}, bf16[512,512]{1,0:T(8,128)(2,1)}) custom-call(bf16[512,7168]{1,0:T(8,128)(2,1)} %tok_ref.1, bf16[512,512]{1,0:T(8,128)(2,1)} %og_ref.3, bf16[2,112,512]{2,1,0:T(8,128)(2,1)} %bitcast.6, f32[28,32,128]{2,1,0:T(8,128)} %bitcast.5, ...), custom_call_target="tpu_custom_call" | custom-call | flops 8000000000 | bytes 24000000 | tf_op jit(solution)/shard_map/pallas_call | solution.py:647
  65.6 8.7 %shard_map.94 = (bf16[512,7168]{1,0:T(8,128)(2,1)}, f32[28,32,128]{2,1,0:T(8,128)}, f32[28,4096]{1,0:T(8,128)}, bf16[512,512]{1,0:T(8,128)(2,1)}) custom-call(bf16[512,512]{1,0:T(8,128)(2,1)} %og_ref.3, bf16[7168,512]{1,0:T(8,128)(2,1)} %bitcast.8, f32[7,2,64,128]{3,2,1,0:T(8,128)} %get-tuple-element.13.mom_ref, ...), custom_call_target="tpu_custom_call" | custom-call | flops 4000000000 | bytes 16000000 | tf_op jit(solution)/shard_map/pallas_call | solution.py:723
